TPU v7x, 256 devices: a whole 4x4x8 slice. The times are simulated.
256 devices in a mesh: dp: 8 (over z), label: 32 (over y, x, core).
Axes of the slice: x: 4, y: 4, z: 8, core: 2. Of those that a mesh axis runs over, the one named last changes fastest.
Arguments:
- token_ids: int32 [16384, 32], P(('dp', 'label')), may hold values from 0 to 30463
- token_table: bfloat16 [30464, 768], P('label'), may hold values from -6 to 6
- norm_gain: float32 [768], replicated, may hold values from 0.1 to 1.9
- slab: bfloat16 [65536, 768], P('label'), may hold values from -0.21875 to 0.21875
- shortlist: int32 [16384, 8], P(('dp', 'label')), may hold values from 0 to 511, all different within a row; in each aligned block of 2048 rows (0 to 2047, 2048 to 4095, ...) at most 96 rows name the same one
- positive_offsets: int32 [16384, 2], P(('dp', 'label')), may hold values from 0 to 127
Outputs:
- embed_grad: float32 [16384, 768], P(('dp', 'label'))
- slab_grad: float32 [2048, 32, 768], P('dp', 'label')
Inputs may be any that keep to these rules, and one draw needn't show every extreme that they name: `shortlist`: each query names 8 different label blocks. In each aligned block of 2048 queries (one index of dp) no label block is named by more than 96 queries, and some label block by exactly 96. `positive_offsets`: positive p of query q lies in the block shortlist[q, p], at this row of it.
All inputs are finite; a program needn't handle non-finite values.
Results may differ from a plain program's by a relative error of at most 0.003.
Values may be sent and summed in bfloat16 or wider, within the bound.
A program may use at most 64 MiB of HBM per device.

v0:
```python
import math

import jax
import jax.numpy as jnp
from jax import lax
from jax.sharding import PartitionSpec as P

K = 8
POS = 2
BLOCK = 128
GCAP = 96


def normalize_rows(pooled, norm_gain):
    scale = lax.rsqrt(jnp.mean(pooled * pooled, axis=-1, keepdims=True) + 1e-06)
    return (pooled * scale * norm_gain).astype(jnp.bfloat16)


def local(token_ids, token_table, norm_gain, slab, shortlist, positive_offsets):
    q_dev, seq_len = token_ids.shape
    vocab_dev, model_width = token_table.shape
    lab_dev = slab.shape[0]
    blk_dev = lab_dev // BLOCK
    owner_index = lax.axis_index("label")
    group_tokens, group_lists, group_pos = (
        lax.all_gather(token_ids, "label", axis=0, tiled=True),
        lax.all_gather(shortlist, "label", axis=0, tiled=True),
        lax.all_gather(positive_offsets, "label", axis=0, tiled=True),
    )
    group_size = group_tokens.shape[0]
    local_words = jnp.arange(vocab_dev, dtype=jnp.int32)

    def count_words(block_tokens):
        word_hits = (block_tokens[:, :, None] == local_words[None, None, :]).astype(jnp.bfloat16)
        return jnp.dot(jnp.sum(word_hits, axis=1), token_table, preferred_element_type=jnp.float32)

    row_count = q_dev * lax.axis_size("label")
    piece_rows = math.gcd(row_count, 256)
    picked = group_tokens - owner_index * vocab_dev
    blocks_in = picked.reshape(row_count // piece_rows, piece_rows, seq_len)
    pooled = (
        lax.psum_scatter(
            lax.map(count_words, blocks_in).reshape(row_count, model_width),
            "label",
            scatter_dimension=0,
            tiled=True,
        )
        / seq_len
    )
    group_embed = lax.all_gather(normalize_rows(pooled, norm_gain), "label", axis=0, tiled=True)
    local_block = (group_lists - owner_index * blk_dev).reshape(-1)
    slot_total = local_block.shape[0]
    block_ids = jnp.arange(blk_dev, dtype=jnp.int32)
    block_hits = (local_block[:, None] == block_ids[None, :]).astype(jnp.int32)
    slot_rank = jnp.sum((jnp.cumsum(block_hits, axis=0) - 1) * block_hits, axis=1)
    is_owned = jnp.sum(block_hits, axis=1) > 0
    slot_place = jnp.where(is_owned, local_block * GCAP + slot_rank, blk_dev * GCAP)
    slot_query = jnp.arange(slot_total, dtype=jnp.int32) // K
    padded_pos = jnp.concatenate(
        [group_pos, jnp.full((group_size, K - POS), -1, jnp.int32)], axis=1
    ).reshape(-1)
    query_table = (
        jnp.full((blk_dev * GCAP + 1,), group_size, jnp.int32)
        .at[slot_place]
        .set(slot_query)[:-1]
        .reshape(blk_dev, GCAP)
    )
    offset_table = (
        jnp.full((blk_dev * GCAP + 1,), -1, jnp.int32)
        .at[slot_place]
        .set(padded_pos)[:-1]
        .reshape(blk_dev, GCAP)
    )
    padded_embed = jnp.concatenate([group_embed, jnp.zeros((1, model_width), jnp.bfloat16)], axis=0)
    slot_embed = jnp.take(padded_embed, query_table, axis=0)
    label_rows = slab.reshape(blk_dev, BLOCK, model_width)
    logits = jnp.einsum("bsd,bid->bsi", slot_embed, label_rows, preferred_element_type=jnp.float32)
    target = (offset_table[:, :, None] == jnp.arange(BLOCK, dtype=jnp.int32)[None, None, :]).astype(
        jnp.float32
    )
    live_slot = (query_table < group_size)[:, :, None]
    grad_logit = jnp.where(live_slot, jax.nn.sigmoid(logits) - target, 0.0).astype(jnp.bfloat16)
    slot_onehot = (
        query_table[:, :, None] == jnp.arange(group_size, dtype=jnp.int32)[None, None, :]
    ).astype(jnp.bfloat16)
    spread = jnp.einsum(
        "bsq,bsi->qbi", slot_onehot, grad_logit, preferred_element_type=jnp.bfloat16
    )
    group_grads = jnp.dot(
        spread.reshape(group_size, lab_dev), slab, preferred_element_type=jnp.float32
    )
    embed_grad = lax.psum_scatter(group_grads, "label", scatter_dimension=0, tiled=True)
    local_part = jnp.einsum(
        "bsi,bsd->bid", grad_logit, slot_embed, preferred_element_type=jnp.float32
    ).reshape(lab_dev, model_width)
    slab_part = lax.psum_scatter(local_part, "dp", scatter_dimension=0, tiled=True)
    return (embed_grad, slab_part.reshape(slab_part.shape[0], 1, model_width))


def solution(mesh):
    return jax.shard_map(
        local,
        mesh=mesh,
        in_specs=(
            P(("dp", "label"), None),
            P("label", None),
            P(),
            P("label", None),
            P(("dp", "label"), None),
            P(("dp", "label"), None),
        ),
        out_specs=(P(("dp", "label"), None), P("dp", "label", None)),
        check_vma=False,
    )
```

profile of v0, /device:TPU:1, one launch (start us, length us, event | category | flops | bytes accessed | tf_op | source)
XLA Modules:
  0.0 578.4 jit_solution(3314242006106851421)
XLA Ops:
  7.2 29.4 %all-gather.1 = s32[32,64,32]{1,2,0:T(8,128)} all-gather(s32[1,64,32]{1,2,0:T(8,128)} %bitcast.73), channel_id=1, replica_groups=mesh['dp'=8,'label'=32] {'label'}, dimensions={0}, use_global_device_ids=true | all-gather | bytes 270336 | tf_op jit(solution)/shard_map/all_gather | solution.py:26
  36.7 1.1 broadcast_subtract_fusion
  37.8 1.1 copy.38
  38.9 1.2 reshape.145
  40.1 55.6 %while.13 = (s32[]{:T(128)}, f32[8,256,768]{2,1,0:T(8,128)}, s32[8,256,32]{1,0,2:T(8,128)S(1)}, bf16[952,768]{1,0:T(8,128)(2,1)}, s32[]{:T(128)}) while((s32[]{:T(128)}, f32[8,256,768]{2,1,0:T(8,128)}, s32[8,256,32]{1,0,2:T(8,128)S(1)}, bf16[952,768]{1,0:T(8,128)(2,1)}, s32[]{:T(128)}) %tuple.38), condition=%wide.region_7.8_spmd.clone, body=%wide.region_5.7_spmd.clone.sunk | while | flops 397494272 | bytes 3387469 | solution.py:43
  40.1 4.0 fusion.46
  44.2 2.9 fusion.47
  47.1 4.0 fusion.46
  51.1 2.9 fusion.47
  54.0 4.0 fusion.46
  58.0 2.9 fusion.47
  61.0 4.0 fusion.46
  65.0 2.9 fusion.47
  67.9 4.0 fusion.46
  71.9 2.9 fusion.47
  74.8 4.0 fusion.46
  78.9 2.9 fusion.47
  81.8 4.0 fusion.46
  85.8 2.9 fusion.47
  88.7 4.0 fusion.46
  92.7 2.9 fusion.47
  95.7 92.2 %reduce-scatter.4.cloned.1.call-done = f32[64,768]{1,0:T(8,128)} async-done(((f32[2048,768]{1,0:T(8,128)}), f32[64,768]{1,0:T(8,128)}) %reduce-scatter.4.cloned.1.call-update) | async-done | bytes 196624 | tf_op jit(solution)/shard_map/reduce_scatter | solution.py:42
  188.0 1.0 multiply_reduce_fusion
  189.0 1.7 multiply_convert_fusion
  190.8 26.3 %all-gather = s32[32,64,8]{1,2,0:T(8,128)S(1)} all-gather(s32[1,64,8]{1,2,0:T(8,128)S(1)} %bitcast.74), channel_id=1, replica_groups=mesh['dp'=8,'label'=32] {'label'}, dimensions={0}, use_global_device_ids=true | all-gather | bytes 67584 | tf_op jit(solution)/shard_map/all_gather | solution.py:27
  217.1 1.3 copy.33
  218.5 1.6 eq.84
  220.1 1.6 eq.80
  221.8 1.3 copy.34
  223.1 1.7 mul.51
  226.4 2.3 add_add_fusion
  228.7 2.6 copy.37
  231.4 2.3 fusion.19
  233.8 60.3 %scatter_custom_fusion = s32[1537]{0:T(1024)S(1)} fusion(s32[16384]{0:T(1024)S(1)} %bitcast.70, s32[16384]{0:T(1024)S(1)} %add_select_fusion, s32[]{:T(128)} %constant.77.clone.1), kind=kCustom, calls=%fused_computation.60 | custom fusion | bytes 6152 | tf_op jit(solution)/shard_map/scatter | solution.py:65
  294.3 21.9 %all-gather.2 = s32[32,64,2]{1,2,0:T(2,128)S(1)} all-gather(s32[1,64,2]{1,2,0:T(2,128)S(1)} %bitcast.75), channel_id=1, replica_groups=mesh['dp'=8,'label'=32] {'label'}, dimensions={0}, use_global_device_ids=true | all-gather | bytes 16896 | tf_op jit(solution)/shard_map/all_gather | solution.py:28
  316.2 1.4 copy.44
  317.6 2.3 concatenate.7.clone
  319.9 1.6 reshape.173
  321.5 60.3 %scatter_custom_fusion.1 = s32[1537]{0:T(1024)S(1)} fusion(s32[16384]{0:T(1024)S(1)} %bitcast.71, s32[16384]{0:T(1024)S(1)} %reshape.173, s32[]{:T(128)} %constant.82.clone.1), kind=kCustom, calls=%fused_computation.57 | custom fusion | bytes 6152 | tf_op jit(solution)/shard_map/scatter | solution.py:71
  382.7 3.8 concatenate.6
  386.4 9.0 %gather_fusion = bf16[1536,768]{1,0:T(8,128)(2,1)} fusion(bf16[2049,768]{1,0:T(8,128)(2,1)} %concatenate.6, s32[2048]{0:T(1024)S(1)} %pad_clamp_fusion), kind=kCustom, calls=%fused_computation | custom fusion | bytes 4724736 | tf_op jit(solution)/shard_map/jit(_take)/gather | solution.py:75
  395.4 2.9 fusion.17
  398.3 3.7 fusion.7
  402.4 3.0 fusion.5
  405.3 9.0 %fusion.32 = f32[2048,768]{1,0:T(8,128)} fusion(bf16[2048,2048]{0,1:T(8,128)(2,1)S(1)} %bitcast.62, bf16[2048,768]{1,0:T(8,128)(2,1)S(1)} %copy-done), kind=kOutput, calls=%fused_computation.65 | convolution fusion | flops 6442450944 | bytes 17825792 | tf_op jit(solution)/shard_map/dot_general | solution.py:89
  414.3 61.8 %reduce-scatter.8.cloned.1.call-done = f32[256,768]{1,0:T(8,128)} async-done(((f32[2048,768]{1,0:T(8,128)}), f32[256,768]{1,0:T(8,128)}) %reduce-scatter.8.cloned.1.call-update) | async-done | bytes 786448 | tf_op jit(solution)/shard_map/reduce_scatter | solution.py:96
  476.1 2.6 reshape.152
  478.7 93.2 %reduce-scatter.6.cloned.1.call-done = f32[64,768]{1,0:T(8,128)} async-done(((f32[2048,768]{1,0:T(8,128)}), f32[64,768]{1,0:T(8,128)}) %reduce-scatter.6.cloned.1.call-update) | async-done | bytes 196624 | tf_op jit(solution)/shard_map/reduce_scatter | solution.py:92
  (55 shorter events, 3.4 us)
Async XLA Ops:
  7.2 388.3 %copy-start = (bf16[2048,768]{1,0:T(8,128)(2,1)S(1)}, bf16[2048,768]{1,0:T(8,128)(2,1)}, u32[]{:S(2)}) copy-start(bf16[2048,768]{1,0:T(8,128)(2,1)} %param.11) | copy-start | bytes 9437188
  7.2 180.8 %reduce-scatter.4.cloned.1.call-start = ((), (), s32[]{:S(2)}) async-start(), calls=%async_computation.3 | async-start | bytes 6488064 | tf_op jit(solution)/shard_map/reduce_scatter | solution.py:42
  95.7 93.4 %copy-start.3 = (f32[768]{0:T(1024)S(1)}, f32[768]{0:T(1024)}, u32[]{:S(2)}) copy-start(f32[768]{0:T(1024)} %param.10) | copy-start | bytes 9220
  95.7 95.1 %copy-start.4 = (s32[64,8]{0,1:T(8,128)S(1)}, s32[64,8]{0,1:T(8,128)}, u32[]{:S(2)}) copy-start(s32[64,8]{0,1:T(8,128)} %param.12) | copy-start | bytes 6148
  95.7 287.0 %all-gather.5.cloned.1.call-start = ((), (), s32[]{:S(2)}) async-start(), calls=%async_computation.4 | async-start | bytes 3244032 | tf_op jit(solution)/shard_map/all_gather | solution.py:50
  190.7 285.4 %reduce-scatter.8.cloned.1.call-start = ((), (), s32[]{:S(2)}) async-start(), calls=%async_computation.6 | async-start | bytes 7077888 | tf_op jit(solution)/shard_map/reduce_scatter | solution.py:96
  225.1 1.0 copy-start.2
  226.2 68.2 %copy-start.5 = (s32[64,2]{0,1:T(2,128)S(1)}, s32[64,2]{0,1:T(2,128)}, u32[]{:S(2)}) copy-start(s32[64,2]{0,1:T(2,128)} %param.13) | copy-start | bytes 1540
  395.4 2.9 copy-start.1
  402.1 169.8 %reduce-scatter.6.cloned.1.call-start = ((), (), s32[]{:S(2)}) async-start(), calls=%async_computation.5 | async-start | bytes 6488064 | tf_op jit(solution)/shard_map/reduce_scatter | solution.py:92
Sparse Core Ops, SparseCore 0:
  95.8 92.1 reduce-scatter.3
  191.4 51.5 all-gather.4
  402.2 73.8 reduce-scatter.7
  481.1 90.7 reduce-scatter.5
where the time goes:
time: 580 us; the launch traced here: 578 us
  waiting for transfers between devices  247 us (43%)
  local copies, waits for them, and re-layouts  156 us (27%)
  blocking collectives  77.6 us (13%)
  matrix products  41.6 us (7%)
  other arithmetic  41.1 us (7%)
  between operations  13.9 us (2%)
    reduce_scatter x1, waiting for transfers between devices, local(): lax.psum_scatter(group_grads, 'label', scatter_dimension=0, tiled=True)  93.2 us
    reduce_scatter x1, waiting for transfers between devices, local(): lax.psum_scatter(lax.map(count_words, blocks_in).reshape(row_count, model...  92.2 us
    reduce_scatter x1, waiting for transfers between devices, local(): lax.psum_scatter(local_part, 'dp', scatter_dimension=0, tiled=True)  61.8 us
    scatter x1, local copies, waits for them, and re-layouts, local(): query_table = jnp.full((blk_dev * GCAP + 1,), group_size, jnp.int32).at[s...  60.3 us
    scatter x1, local copies, waits for them, and re-layouts, local(): offset_table = jnp.full((blk_dev * GCAP + 1,), -1, jnp.int32).at[slot_pla...  60.3 us
    reduce_sum x8, other arithmetic, count_words(): jnp.sum(word_hits, axis=1)  32.1 us
    all_gather x1, blocking collectives, local(): lax.all_gather(token_ids, 'label', axis=0, tiled=True)  29.4 us
    all_gather x1, blocking collectives, local(): lax.all_gather(shortlist, 'label', axis=0, tiled=True)  26.3 us
  transfers between devices with their start and end apart: 4, of which 3 were waited for; matrix products, arithmetic and copies ran while one was open for 27% of the time, Pallas kernels for 0%

commit v1 on v0

v1 whole, which is shorter than its diff:
```python
import functools

import jax
import jax.numpy as jnp
from jax import lax
from jax.experimental import pallas as pl
from jax.experimental.pallas import tpu as pltpu
from jax.sharding import PartitionSpec as P

K = 8
POS = 2
BLOCK = 128
GCAP = 96
SEQ = 32
NX = 4
NY = 4
NZ = 8
CHIPS = NX * NY
Q_DEV = 64
Q_CHIP = 2 * Q_DEV
GROUP = CHIPS * Q_CHIP
VOC = 952
VOC_PAD = 960
LO = 192
FIELDS = 5
D = 768
BLKS = 16
SLOTS = BLKS * GCAP
HALF = Q_DEV // 2
INFO = 48
MESH = pl.DeviceIdType.MESH
F32 = jnp.float32
BF16 = jnp.bfloat16


def kernel(
    tok_ref, list_ref, pos_ref, gain_ref, table_hbm, slab_hbm,
    eg_ref, sg_ref,
    table, slab, stage, sib_info, my_info, info, lo_ref, w_ref, ct, tmp,
    s_own, s_send, s_recv, r_x, r_y, acc_x, acc_y,
    emb, rank, off2, onehot, slot_off, eslots, hgrad,
    zpart, zsend, zrecv,
    g_send, g_recv, gx_send, gx_recv, gy_recv,
    load_sem, info_s, info_r, pair_s, pair_r, rx_s, rx_r, ry_s, ry_r,
    ex_s, ex_r, ey_s, ey_r, es_s, es_r, z_s, z_r,
    gp_s, gp_r, gx_s, gx_r, gy_s, gy_r,
):
    z = lax.axis_index("dp")
    label = lax.axis_index("label")
    y = lax.div(label, 2 * NX)
    x = lax.rem(lax.div(label, 2), NX)
    c = lax.rem(label, 2)
    o = 1 - c

    def lab(yy, xx, cc):
        return (yy * NX + xx) * 2 + cc

    def at_x(dx):
        return (z, lab(y, lax.rem(x + dx, NX), c))

    def at_y(dy):
        return (z, lab(lax.rem(y + dy, NY), x, c))

    sibling = (z, lab(y, x, o))
    up = (lax.rem(z + 1, NZ), label)
    down = (lax.rem(z + NZ - 1, NZ), label)

    def send(src, dst, ssem, rsem, device):
        copy = pltpu.make_async_remote_copy(
            src_ref=src, dst_ref=dst, send_sem=ssem, recv_sem=rsem,
            device_id=device, device_id_type=MESH,
        )
        copy.start()
        return copy

    load_table = pltpu.make_async_copy(table_hbm, table.at[pl.ds(0, VOC)], load_sem.at[0])
    load_slab = pltpu.make_async_copy(slab_hbm, slab, load_sem.at[1])
    load_table.start()
    load_slab.start()

    barrier = pltpu.get_barrier_semaphore()
    peers = [sibling, up, down] + [at_x(d) for d in (1, 2, 3)] + [at_y(d) for d in (1, 2, 3)]
    for device in peers:
        pl.semaphore_signal(barrier, inc=1, device_id=device, device_id_type=MESH)

    stage[...] = jnp.zeros_like(stage)
    mine_rows = pl.ds(pl.multiple_of(c * Q_DEV, Q_DEV), Q_DEV)
    stage[mine_rows, 0:SEQ] = tok_ref[...]
    stage[mine_rows, SEQ : SEQ + K] = list_ref[...]
    stage[mine_rows, SEQ + K : SEQ + K + POS] = pos_ref[...]
    mine = stage[...].T[0:INFO, :]
    my_info[...] = mine.astype(jnp.int16)
    pl.semaphore_wait(barrier, len(peers))

    pending = []
    first = send(my_info, sib_info, info_s.at[0], info_r.at[0], sibling)
    load_table.wait()
    table[VOC:VOC_PAD, :] = jnp.zeros((VOC_PAD - VOC, D), BF16)
    first.wait()
    info[y, x] = (mine + sib_info[...].astype(jnp.int32)).astype(jnp.int16)
    copies = [
        send(info.at[y, x], info.at[y, x], info_s.at[d], info_r.at[d], at_x(d)) for d in (2, 1, 3)
    ]
    for copy in copies:
        copy.wait()
    copies = [
        send(info.at[y], info.at[y], info_s.at[3 + d], info_r.at[3 + d], at_y(d)) for d in (2, 1, 3)
    ]
    for copy in copies:
        copy.wait()

    base = label * VOC
    half_lo = LO // 2

    def pool_pair(pair, carry):
        for side in range(2):
            j = pair * 2 + side
            ids = info[lax.div(j, NX), lax.rem(j, NX), 0:SEQ, :].astype(jnp.int32) - base
            valid = (ids >= 0) & (ids < VOC)
            high = (ids * 683) >> 17
            weight = jnp.ones_like(ids)
            for f in range(1, FIELDS):
                weight = jnp.where(high == f, 1 << (6 * f), weight)
            lo_ref[...] = jnp.where(valid, ids - high * LO, -1)
            w_ref[...] = jnp.where(valid, weight, 0)
            for part in range(2):
                rows = lax.broadcasted_iota(jnp.int32, (half_lo, 128), 0) + part * half_lo
                acc = jnp.zeros((half_lo, 128), jnp.int32)
                for t in range(SEQ):
                    acc = acc + jnp.where(lo_ref[t : t + 1, :] == rows, w_ref[t : t + 1, :], 0)
                for f in range(FIELDS):
                    field = (acc >> (6 * f)) & 63
                    ct[pl.ds(f * LO + part * half_lo, half_lo), pl.ds(side * 128, 128)] = (
                        field.astype(F32).astype(BF16)
                    )
        pooled = lax.dot_general(
            ct[...], table[...], (((0,), (0,)), ((), ())), preferred_element_type=F32
        )
        tmp[...] = pooled.reshape(4, Q_DEV, D)
        for side in range(2):
            s_own[pair * 2 + side] = tmp[side * 2 + c].reshape(2, HALF, D)
            s_send[pair * 2 + side] = tmp[side * 2 + o].reshape(2, HALF, D)
        at = pl.ds(pair * 2, 2)
        send(s_send.at[at], s_recv.at[at], pair_s.at[pair], pair_r.at[pair], sibling)
        return carry

    lax.fori_loop(0, CHIPS // 2, pool_pair, 0)

    def pair_wait(pair, carry):
        at = pl.ds(pair * 2, 2)
        pltpu.make_async_remote_copy(
            src_ref=s_send.at[at], dst_ref=s_recv.at[at], send_sem=pair_s.at[pair],
            recv_sem=pair_r.at[pair], device_id=sibling, device_id_type=MESH,
        ).wait()
        for side in range(2):
            j = pair * 2 + side
            both = s_own[j] + s_recv[j]
            acc_x[lax.rem(j, NX), lax.div(j, NX)] = both[0]
            acc_y[lax.div(j, NX), lax.rem(j, NX)] = both[1]
        return carry

    lax.fori_loop(0, CHIPS // 2, pair_wait, 0)

    copies_x = {
        d: send(acc_x.at[lax.rem(x + d, NX)], r_x.at[0, d - 1], rx_s.at[0, d - 1], rx_r.at[0, d - 1], at_x(d))
        for d in (2, 1, 3)
    }
    copies_y = {
        d: send(acc_y.at[lax.rem(y + d, NY)], r_x.at[1, d - 1], rx_s.at[1, d - 1], rx_r.at[1, d - 1], at_y(d))
        for d in (2, 1, 3)
    }

    before = (
        lax.broadcasted_iota(jnp.int32, (128, 128), 0) < lax.broadcasted_iota(jnp.int32, (128, 128), 1)
    ).astype(F32).astype(BF16)
    ones = jnp.ones((128, 128), BF16)
    block_ids = lax.broadcasted_iota(jnp.int32, (BLKS, 128), 0) + label * BLKS
    running = jnp.zeros((BLKS, 128), F32)
    for j in range(CHIPS):
        lists = info[j // NX, j % NX, SEQ:INFO, :].astype(jnp.int32)
        hit = jnp.zeros((BLKS, 128), F32)
        place = jnp.zeros((BLKS, 128), F32)
        for k in range(K):
            same = lists[k : k + 1, :] == block_ids
            hit = hit + jnp.where(same, 1.0, 0.0)
            if k < POS:
                at_row = lists[K + k : K + k + 1, :].astype(F32) + 1.0
                place = place + jnp.where(same, at_row, 0.0)
        hit16 = hit.astype(BF16)
        ahead = jnp.dot(hit16, before, preferred_element_type=F32) + running
        running = running + jnp.dot(hit16, ones, preferred_element_type=F32)
        rank[:, j, :] = jnp.where(hit > 0.0, ahead, -1.0)
        off2[:, j, :] = hit + place

    slot_ids = lax.broadcasted_iota(jnp.int32, (GCAP, 128), 0).astype(F32)

    def one_hot(b, carry):
        rows = pl.ds(pl.multiple_of(b * GCAP, GCAP), GCAP)
        found = jnp.zeros((GCAP, 128), F32)
        for j in range(CHIPS):
            lanes = slice(j * 128, (j + 1) * 128)
            same = rank[b, j : j + 1, :] == slot_ids
            onehot[rows, lanes] = jnp.where(same, 1.0, 0.0).astype(BF16)
            found = found + jnp.where(same, off2[b, j : j + 1, :], 0.0)
        slot_off[rows, :] = jnp.broadcast_to(jnp.sum(found, axis=1, keepdims=True), (GCAP, 128))
        return carry

    lax.fori_loop(0, BLKS, one_hot, 0)

    for d in (1, 3, 2):
        copies_x[d].wait()
        copies_y[d].wait()
    acc_x[x] = acc_x[x] + r_x[0, 0] + r_x[0, 1] + r_x[0, 2]
    acc_y[y] = acc_y[y] + r_x[1, 0] + r_x[1, 1] + r_x[1, 2]
    copies = []
    for d in (2, 1, 3):
        yy, xx = lax.rem(y + d, NY), lax.rem(x + d, NX)
        copies.append(send(acc_x.at[x, yy], r_y.at[0, d - 1], ry_s.at[0, d - 1], ry_r.at[0, d - 1], at_y(d)))
        copies.append(send(acc_y.at[y, xx], r_y.at[1, d - 1], ry_s.at[1, d - 1], ry_r.at[1, d - 1], at_x(d)))
    for copy in copies:
        copy.wait()
    gain = gain_ref[...]
    for half in range(2):
        mine_sum = acc_x[x, y] if half == 0 else acc_y[y, x]
        pooled = (mine_sum + r_y[half, 0] + r_y[half, 1] + r_y[half, 2]) / SEQ
        scale = lax.rsqrt(jnp.mean(pooled * pooled, axis=-1, keepdims=True) + 1e-06)
        emb[y, x, c, half] = (pooled * scale * gain).astype(BF16)

    ex = {}
    for d in (2, 1, 3):
        ex[0, d] = send(emb.at[y, x, c, 0], emb.at[y, x, c, 0], ex_s.at[0, d - 1], ex_r.at[0, d - 1], at_x(d))
        ex[1, d] = send(emb.at[y, x, c, 1], emb.at[y, x, c, 1], ex_s.at[1, d - 1], ex_r.at[1, d - 1], at_y(d))
    for d in (1, 3, 2):
        ex[0, d].wait()
        ex[1, d].wait()
    row = emb.at[y, :, c, 0]
    col = emb.at[:, x, c, 1]
    ey = {}
    for d in (2, 1, 3):
        ey[0, d] = send(row, row, ey_s.at[0, d - 1], ey_r.at[0, d - 1], at_y(d))
        ey[1, d] = send(col, col, ey_s.at[1, d - 1], ey_r.at[1, d - 1], at_x(d))
    es = [
        send(row, row, es_s.at[0, 0], es_r.at[0, 0], sibling),
        send(col, col, es_s.at[1, 0], es_r.at[1, 0], sibling),
    ]
    load_slab.wait()
    for d in (1, 3, 2):
        ey[0, d].wait()
        ey[1, d].wait()
        row = emb.at[lax.rem(y + NY - d, NY), :, c, 0]
        col = emb.at[:, lax.rem(x + NX - d, NX), c, 1]
        es.append(send(row, row, es_s.at[0, d], es_r.at[0, d], sibling))
        es.append(send(col, col, es_s.at[1, d], es_r.at[1, d], sibling))
    for copy in es:
        copy.wait()

    def gather_slots(m, carry):
        rows = pl.ds(pl.multiple_of(m * 768, 768), 768)
        eslots[rows, :] = jnp.dot(
            onehot[rows, :], emb[...].reshape(GROUP, D), preferred_element_type=F32
        ).astype(BF16)
        return carry

    lax.fori_loop(0, SLOTS // 768, gather_slots, 0)

    pair_rows = 2 * GCAP
    row_ids = lax.broadcasted_iota(jnp.int32, (pair_rows, 2 * BLOCK), 0)
    col_ids = lax.broadcasted_iota(jnp.int32, (pair_rows, 2 * BLOCK), 1)
    same_block = (row_ids >= GCAP) == (col_ids >= BLOCK)
    col_in = jnp.where(col_ids >= BLOCK, col_ids - BLOCK, col_ids).astype(F32) + 2.0

    def grads(offset):
        dest = lax.rem(z + offset + NZ, NZ)
        srows = pl.ds(pl.multiple_of(dest * pair_rows, pair_rows), pair_rows)
        lrows = pl.ds(pl.multiple_of(dest * 2 * BLOCK, 2 * BLOCK), 2 * BLOCK)
        es_rows = eslots[srows, :]
        labels = slab[lrows, :]
        logits = lax.dot_general(es_rows, labels, (((1,), (1,)), ((), ())), preferred_element_type=F32)
        seen = slot_off[srows, :]
        seen = jnp.concatenate([seen, seen], axis=1)
        g = jax.nn.sigmoid(logits) - jnp.where(seen == col_in, 1.0, 0.0)
        g = jnp.where(same_block & (seen > 0.0), g, 0.0).astype(BF16)
        hgrad[srows, :] = jnp.dot(g, labels, preferred_element_type=F32).astype(BF16)
        return lax.dot_general(g, es_rows, (((0,), (0,)), ((), ())), preferred_element_type=F32)

    zc = {}

    def z_send(way, step, sub):
        zc[way, step, sub] = send(
            zsend.at[way, step, sub], zrecv.at[way, step, sub],
            z_s.at[way, step, sub], z_r.at[way, step, sub], up if way == 0 else down,
        )

    def z_fill(way, step, sub, with_recv):
        value = zpart[way, step - 1, pl.ds(sub * BLOCK, BLOCK), :]
        if with_recv:
            value = value + zrecv[way, step - 1, sub].astype(F32)
        zsend[way, step, sub] = value.astype(BF16)
        z_send(way, step, sub)

    far = grads(4)
    for way in range(2):
        zsend[way, 0, way] = far[way * BLOCK : (way + 1) * BLOCK, :].astype(BF16)
        z_send(way, 0, way)
    for way, sign in ((0, 1), (1, -1)):
        zpart[way, 0] = grads(3 * sign)
        z_fill(way, 1, 1 - way, False)
    for way in range(2):
        zc[way, 0, way].wait()
        z_fill(way, 1, way, True)
    for step in (2, 3):
        for way, sign in ((0, 1), (1, -1)):
            zpart[way, step - 1] = grads((4 - step) * sign)
    own_part = grads(0)
    sg_ref[...] = own_part
    for way in range(2):
        zc[way, 1, 1 - way].wait()
        z_fill(way, 2, 1 - way, True)
    for way in range(2):
        zc[way, 1, way].wait()
        z_fill(way, 2, way, True)

    def spread_pair(pair, carry):
        lanes = pl.ds(pl.multiple_of(pair * 256, 256), 256)
        grad = lax.dot_general(
            onehot[:, lanes], hgrad[...], (((0,), (0,)), ((), ())), preferred_element_type=F32
        )
        tmp[...] = grad.reshape(4, Q_DEV, D)
        for side in range(2):
            s_own[pair * 2 + side] = tmp[side * 2 + c].reshape(2, HALF, D)
            g_send[pair * 2 + side] = tmp[side * 2 + o].astype(BF16)
        at = pl.ds(pair * 2, 2)
        send(g_send.at[at], g_recv.at[at], gp_s.at[pair], gp_r.at[pair], sibling)
        return carry

    lax.fori_loop(0, CHIPS // 2, spread_pair, 0)

    for sub_of in (1, 0):
        for way in range(2):
            sub = 1 - way if sub_of else way
            zc[way, 2, sub].wait()
            z_fill(way, 3, sub, True)

    def grad_pair_wait(pair, carry):
        at = pl.ds(pair * 2, 2)
        pltpu.make_async_remote_copy(
            src_ref=g_send.at[at], dst_ref=g_recv.at[at], send_sem=gp_s.at[pair],
            recv_sem=gp_r.at[pair], device_id=sibling, device_id_type=MESH,
        ).wait()
        for side in range(2):
            j = pair * 2 + side
            both = s_own[j] + g_recv[j].astype(F32).reshape(2, HALF, D)
            xx, yy = lax.rem(j, NX), lax.div(j, NX)
            acc_x[xx, yy] = both[0]
            acc_y[yy, xx] = both[1]
            gx_send[0, xx, yy] = both[0].astype(BF16)
            gx_send[1, yy, xx] = both[1].astype(BF16)
        return carry

    lax.fori_loop(0, CHIPS // 2, grad_pair_wait, 0)

    copies = []
    for d in (2, 1, 3):
        copies.append(send(gx_send.at[0, lax.rem(x + d, NX)], gx_recv.at[0, d - 1], gx_s.at[0, d - 1], gx_r.at[0, d - 1], at_x(d)))
        copies.append(send(gx_send.at[1, lax.rem(y + d, NY)], gx_recv.at[1, d - 1], gx_s.at[1, d - 1], gx_r.at[1, d - 1], at_y(d)))
    for copy in copies:
        copy.wait()
    acc_x[x] = acc_x[x] + sum(gx_recv[0, i].astype(F32) for i in range(3))
    acc_y[y] = acc_y[y] + sum(gx_recv[1, i].astype(F32) for i in range(3))
    copies = []
    for d in (2, 1, 3):
        yy, xx = lax.rem(y + d, NY), lax.rem(x + d, NX)
        copies.append(send(acc_x.at[x, yy], gy_recv.at[0, d - 1], gy_s.at[0, d - 1], gy_r.at[0, d - 1], at_y(d)))
        copies.append(send(acc_y.at[y, xx], gy_recv.at[1, d - 1], gy_s.at[1, d - 1], gy_r.at[1, d - 1], at_x(d)))
    for sub in range(2):
        rows = pl.ds(sub * BLOCK, BLOCK)
        for way in range(2):
            zc[way, 3, sub].wait()
        sg_ref[rows, :] = sg_ref[rows, :] + zrecv[0, 3, sub].astype(F32) + zrecv[1, 3, sub].astype(F32)
    for copy in copies:
        copy.wait()
    eg_ref[0:HALF, :] = acc_x[x, y] + gy_recv[0, 0] + gy_recv[0, 1] + gy_recv[0, 2]
    eg_ref[HALF:Q_DEV, :] = acc_y[y, x] + gy_recv[1, 0] + gy_recv[1, 1] + gy_recv[1, 2]


def local(token_ids, token_table, norm_gain, slab, shortlist, positive_offsets):
    vmem = pl.BlockSpec(memory_space=pltpu.VMEM)
    anyspace = pl.BlockSpec(memory_space=pl.ANY)
    dma = pltpu.SemaphoreType.DMA
    scratch = dict(
        table=pltpu.VMEM((VOC_PAD, D), BF16),
        slab=pltpu.VMEM((BLKS * BLOCK, D), BF16),
        stage=pltpu.VMEM((128, 128), jnp.int32),
        sib_info=pltpu.VMEM((INFO, 128), jnp.int16),
        my_info=pltpu.VMEM((INFO, 128), jnp.int16),
        info=pltpu.VMEM((NY, NX, INFO, 128), jnp.int16),
        lo_ref=pltpu.VMEM((SEQ, 128), jnp.int32),
        w_ref=pltpu.VMEM((SEQ, 128), jnp.int32),
        ct=pltpu.VMEM((VOC_PAD, 256), BF16),
        tmp=pltpu.VMEM((4, Q_DEV, D), F32),
        s_own=pltpu.VMEM((CHIPS, 2, HALF, D), F32),
        s_send=pltpu.VMEM((CHIPS, 2, HALF, D), F32),
        s_recv=pltpu.VMEM((CHIPS, 2, HALF, D), F32),
        r_x=pltpu.VMEM((2, 3, NY, HALF, D), F32),
        r_y=pltpu.VMEM((2, 3, HALF, D), F32),
        acc_x=pltpu.VMEM((NX, NY, HALF, D), F32),
        acc_y=pltpu.VMEM((NY, NX, HALF, D), F32),
        emb=pltpu.VMEM((NY, NX, 2, 2, HALF, D), BF16),
        rank=pltpu.VMEM((BLKS, CHIPS, 128), F32),
        off2=pltpu.VMEM((BLKS, CHIPS, 128), F32),
        onehot=pltpu.VMEM((SLOTS, GROUP), BF16),
        slot_off=pltpu.VMEM((SLOTS, 128), F32),
        eslots=pltpu.VMEM((SLOTS, D), BF16),
        hgrad=pltpu.VMEM((SLOTS, D), BF16),
        zpart=pltpu.VMEM((2, 3, 2 * BLOCK, D), F32),
        zsend=pltpu.VMEM((2, 4, 2, BLOCK, D), BF16),
        zrecv=pltpu.VMEM((2, 4, 2, BLOCK, D), BF16),
        g_send=pltpu.VMEM((CHIPS, Q_DEV, D), BF16),
        g_recv=pltpu.VMEM((CHIPS, Q_DEV, D), BF16),
        gx_send=pltpu.VMEM((2, 4, 4, HALF, D), BF16),
        gx_recv=pltpu.VMEM((2, 3, 4, HALF, D), BF16),
        gy_recv=pltpu.VMEM((2, 3, HALF, D), F32),
        load_sem=dma((2,)),
        info_s=dma((7,)), info_r=dma((7,)),
        pair_s=dma((CHIPS // 2,)), pair_r=dma((CHIPS // 2,)),
        rx_s=dma((2, 3)), rx_r=dma((2, 3)), ry_s=dma((2, 3)), ry_r=dma((2, 3)),
        ex_s=dma((2, 3)), ex_r=dma((2, 3)), ey_s=dma((2, 3)), ey_r=dma((2, 3)),
        es_s=dma((2, 4)), es_r=dma((2, 4)),
        z_s=dma((2, 4, 2)), z_r=dma((2, 4, 2)),
        gp_s=dma((CHIPS // 2,)), gp_r=dma((CHIPS // 2,)),
        gx_s=dma((2, 3)), gx_r=dma((2, 3)), gy_s=dma((2, 3)), gy_r=dma((2, 3)),
    )
    eg, sg = pl.pallas_call(
        kernel,
        out_shape=(
            jax.ShapeDtypeStruct((Q_DEV, D), F32),
            jax.ShapeDtypeStruct((2 * BLOCK, D), F32),
        ),
        in_specs=[vmem, vmem, vmem, vmem, anyspace, anyspace],
        out_specs=(vmem, vmem),
        scratch_shapes=list(scratch.values()),
        compiler_params=pltpu.CompilerParams(
            collective_id=0, has_side_effects=True, vmem_limit_bytes=63 << 20
        ),
    )(token_ids, shortlist, positive_offsets, norm_gain.reshape(1, D), token_table, slab)
    return eg, sg.reshape(2 * BLOCK, 1, D)


def solution(mesh):
    return jax.shard_map(
        local,
        mesh=mesh,
        in_specs=(
            P(("dp", "label"), None),
            P("label", None),
            P(),
            P("label", None),
            P(("dp", "label"), None),
            P(("dp", "label"), None),
        ),
        out_specs=(P(("dp", "label"), None), P("dp", "label", None)),
        check_vma=False,
    )
```

time: 580 us -> 137 us (0.24)
  waiting for transfers between devices: 247 us -> 0 us
  local copies, waits for them, and re-layouts: 156 us -> 9.89 us
  Pallas kernels: 0 us -> 126 us
  blocking collectives: 77.6 us -> 0 us
  matrix products: 41.6 us -> 0 us
  other arithmetic: 41.1 us -> 0 us
  between operations: 13.9 us -> 0.64 us
    reduce_scatter x3 -> x0, waiting for transfers between devices: 247 us -> none  [the longest x1 93.2 us: local(): lax.psum_scatter(group_grads, 'label', scatter_dimension=0, tiled=True)]
    pallas_call x0 -> x1, Pallas kernels: none -> 126 us  [local(): pl.pallas_call(kernel, out_shape=(jax.ShapeDtypeStruct((Q_DEV, D), F32),...]
    scatter x2 -> x0, local copies, waits for them, and re-layouts: 121 us -> none  [the longest x1 60.3 us: local(): query_table = jnp.full((blk_dev * GCAP + 1,), group_size, jnp.int32).at[s...]
    all_gather x3 -> x0, blocking collectives: 77.6 us -> none  [the longest x1 29.4 us: local(): lax.all_gather(token_ids, 'label', axis=0, tiled=True)]
    dot_general x12 -> x0, matrix products: 41.6 us -> none  [the longest x8 23.1 us: count_words(): jnp.dot(jnp.sum(word_hits, axis=1), token_table, preferred_element_type=j...]
    reduce_sum x10 -> x0, other arithmetic: 35.4 us -> none  [the longest x8 32.1 us: count_words(): jnp.sum(word_hits, axis=1)]
    gather x1 -> x0, local copies, waits for them, and re-layouts: 9 us -> none  [local(): slot_embed = jnp.take(padded_embed, query_table, axis=0)]
    unnamed x13 -> x5, local copies, waits for them, and re-layouts: 2.46 us -> 8.61 us
  transfers between devices with their start and end apart: 4 -> 0, of which waited for: 3 -> 0; matrix products, arithmetic and copies ran while one was open for 27% -> 0% of each run, Pallas kernels for 0% -> 0%
where the time goes in v1:
time: 137 us
  Pallas kernels  126 us (92%)
  local copies, waits for them, and re-layouts  9.89 us (7%)
    pallas_call x1, Pallas kernels, local(): pl.pallas_call(kernel, out_shape=(jax.ShapeDtypeStruct((Q_DEV, D), F32),...  126 us
    unnamed x5, local copies, waits for them, and re-layouts  8.61 us

profile of v1, /device:TPU:1, one launch (start us, length us, event | category | flops | bytes accessed | tf_op | source)
XLA Modules:
  0.0 136.9 jit_solution(12461399173552034518)
XLA Ops:
  0.6 1.3 reshape.10.gain_ref
  1.9 1.4 %copy.8.tok_ref = s32[64,32]{1,0:T(8,128)} copy(s32[64,32]{0,1:T(8,128)} %param.6) | data formatting | bytes 16384 | tf_op args[0]
  3.3 1.4 %copy.9.list_ref = s32[64,8]{1,0:T(8,128)} copy(s32[64,8]{0,1:T(8,128)} %param.10) | data formatting | bytes 4096 | tf_op args[4]
  4.7 1.4 %copy.10.pos_ref = s32[64,2]{1,0:T(8,128)} copy(s32[64,2]{0,1:T(2,128)} %param.11) | data formatting | bytes 1024 | tf_op args[5]
  6.1 126.4 %shard_map.77 = (f32[64,768]{1,0:T(8,128)}, f32[256,768]{1,0:T(8,128)}) custom-call(s32[64,32]{1,0:T(8,128)} %copy.8.tok_ref, s32[64,8]{1,0:T(8,128)} %copy.9.list_ref, s32[64,2]{1,0:T(8,128)} %copy.10.pos_ref, f32[1,768]{1,0:T(1,128)} %reshape.10.gain_ref, bf16[952,768]{1,0:T(8,128)(2,1)} %table_hbm.1, bf16[2048,768]{1,0:T(8,128)(2,1)} %slab_hbm.1), custom_call_target="tpu_custom_call" | custom-call | tf_op jit(solution)/shard_map/pallas_call | solution.py:433
  132.5 2.8 %copy.11 = f32[256,1,768]{2,1,0:T(1,128)} copy(f32[256,1,768]{2,0,1:T(8,128)} %bitcast.1) | data formatting | bytes 1572864
  135.3 1.6 %copy.13 = f32[64,768]{1,0:T(8,128)} copy(f32[64,768]{1,0:T(8,128)} %get-tuple-element.10) | data formatting | bytes 393216

commit v2 on v1

v2 whole, which is shorter than its diff:
```python
import math

import jax
import jax.numpy as jnp
from jax import lax
from jax.experimental import pallas as pl
from jax.experimental.pallas import tpu as pltpu
from jax.sharding import PartitionSpec as P

K = 8
POS = 2
BLOCK = 128
GCAP = 96
SEQ = 32
NX = 4
NY = 4
NZ = 8
CHIPS = NX * NY
Q_DEV = 64
Q_CHIP = 2 * Q_DEV
GROUP = CHIPS * Q_CHIP
VOC = 952
VOC_PAD = 960
LO = 192
FIELDS = 5
D = 768
BLKS = 16
SLOTS = BLKS * GCAP
HALF = Q_DEV // 2
INFO = 48
TILES = 8
TILE = 256
Q_COLS = D + 128
TOP = 32000.0
MESH = pl.DeviceIdType.MESH
F32 = jnp.float32
BF16 = jnp.bfloat16


def pack_rows(value, dst):
    largest = jnp.max(jnp.abs(value), axis=-1, keepdims=True)
    step = jnp.ceil(jnp.log(jnp.maximum(largest, 1e-30)) * (8.0 / math.log(2.0)))
    factor = jnp.exp(step * (-math.log(2.0) / 8.0)) * TOP
    dst[:, 0:D] = jnp.round(value * factor).astype(jnp.int32).astype(jnp.int16)
    dst[:, D:Q_COLS] = jnp.broadcast_to(step, (value.shape[0], 128)).astype(jnp.int32).astype(jnp.int16)


def unpack_rows(src):
    step = src[:, D : D + 1].astype(jnp.int32).astype(F32)
    factor = jnp.exp(step * (math.log(2.0) / 8.0)) * (1.0 / TOP)
    return src[:, 0:D].astype(jnp.int32).astype(F32) * factor


def kernel(
    tok_ref, list_ref, pos_ref, gain_ref, table_hbm, slab_hbm,
    eg_ref, sg_ref,
    table, slab, stage, sib_info, my_info, info, lo_ref, w_ref, ct, tmp,
    s_own, s_send, s_recv, qa, ra, qb, rb, qa2, ra2, qb2, rb2, acc_a, acc_b,
    emb, rank, off2, onehot, slot_off, eacc, eslots, hgrad,
    zpart, zsend, zrecv,
    g_own, g_send, g_recv, gx_send, gx_recv, gy_send, gy_recv,
    load_sem, info_s, info_r, pair_s, pair_r, ra_s, ra_r, rb_s, rb_r, r2_s, r2_r,
    ex_s, ex_r, ey_s, ey_r, es_s, es_r, z_s, z_r,
    gp_s, gp_r, gx_s, gx_r, gy_s, gy_r,
):
    z = lax.axis_index("dp")
    label = lax.axis_index("label")
    y = lax.div(label, 2 * NX)
    x = lax.rem(lax.div(label, 2), NX)
    c = lax.rem(label, 2)
    o = 1 - c

    def lab(yy, xx, cc):
        return (yy * NX + xx) * 2 + cc

    def at_x(dx):
        return (z, lab(y, lax.rem(x + dx, NX), c))

    def at_y(dy):
        return (z, lab(lax.rem(y + dy, NY), x, c))

    sibling = (z, lab(y, x, o))
    up = (lax.rem(z + 1, NZ), label)
    down = (lax.rem(z + NZ - 1, NZ), label)

    def send(src, dst, ssem, rsem, device):
        copy = pltpu.make_async_remote_copy(
            src_ref=src, dst_ref=dst, send_sem=ssem, recv_sem=rsem,
            device_id=device, device_id_type=MESH,
        )
        copy.start()
        return copy

    load_table = pltpu.make_async_copy(table_hbm, table.at[pl.ds(0, VOC)], load_sem.at[0])
    load_slab = pltpu.make_async_copy(slab_hbm, slab, load_sem.at[1])
    load_table.start()
    load_slab.start()

    barrier = pltpu.get_barrier_semaphore()
    peers = [sibling, up, down] + [at_x(d) for d in (1, 2, 3)] + [at_y(d) for d in (1, 2, 3)]
    for device in peers:
        pl.semaphore_signal(barrier, inc=1, device_id=device, device_id_type=MESH)

    stage[...] = jnp.zeros_like(stage)
    for core in range(2):

        @pl.when(c == core)
        def _():
            for half in range(2):
                src = slice(half * HALF, (half + 1) * HALF)
                dst = slice(half * Q_DEV + core * HALF, half * Q_DEV + (core + 1) * HALF)
                stage[0:SEQ, dst] = tok_ref[:, src]
                stage[SEQ : SEQ + K, dst] = list_ref[:, src]
                stage[SEQ + K : SEQ + K + POS, dst] = pos_ref[:, src]

    mine = stage[...]
    my_info[...] = mine.astype(jnp.int16)
    pl.semaphore_wait(barrier, len(peers))

    first = send(my_info, sib_info, info_s.at[0], info_r.at[0], sibling)
    load_table.wait()
    table[VOC:VOC_PAD, :] = jnp.zeros((VOC_PAD - VOC, D), BF16)
    first.wait()
    info[y, x] = (mine + sib_info[...].astype(jnp.int32)).astype(jnp.int16)
    copies = [
        send(info.at[y, x], info.at[y, x], info_s.at[d], info_r.at[d], at_x(d)) for d in (2, 1, 3)
    ]
    for copy in copies:
        copy.wait()
    info_y = {
        d: send(info.at[y], info.at[y], info_s.at[3 + d], info_r.at[3 + d], at_y(d)) for d in (2, 1, 3)
    }

    base = label * VOC
    half_lo = LO // 2
    row_steps = (0, 2, 1, 3)
    pair_copies = {}
    ra_copies, rb_copies = {}, {}

    def pool_row(i):
        r = lax.rem(y + row_steps[i], NY)

        def pool_pair(pair, carry):
            for side in range(2):
                ids = info[r, pair * 2 + side, 0:SEQ, :].astype(jnp.int32) - base
                valid = (ids >= 0) & (ids < VOC)
                high = (ids * 683) >> 17
                weight = jnp.ones_like(ids)
                for f in range(1, FIELDS):
                    weight = jnp.where(high == f, 1 << (6 * f), weight)
                lo_ref[...] = jnp.where(valid, ids - high * LO, -1)
                w_ref[...] = jnp.where(valid, weight, 0)
                for part in range(2):
                    rows = lax.broadcasted_iota(jnp.int32, (half_lo, 128), 0) + part * half_lo
                    acc = jnp.zeros((half_lo, 128), jnp.int32)
                    for t in range(SEQ):
                        acc = acc + jnp.where(lo_ref[t : t + 1, :] == rows, w_ref[t : t + 1, :], 0)
                    for f in range(FIELDS):
                        field = (acc >> (6 * f)) & 63
                        ct[pl.ds(f * LO + part * half_lo, half_lo), pl.ds(side * 128, 128)] = (
                            field.astype(F32).astype(BF16)
                        )
            pooled = lax.dot_general(
                ct[...], table[...], (((0,), (0,)), ((), ())), preferred_element_type=F32
            )
            tmp[...] = pooled.reshape(4, 2, HALF, D)
            for side in range(2):
                for half in range(2):
                    s_own[i, pair * 2 + side, half] = tmp[side * 2 + half, c]
                    s_send[i, pair * 2 + side, half] = tmp[side * 2 + half, o]
            at = pl.ds(pair * 2, 2)
            send(s_send.at[i, at], s_recv.at[i, at], pair_s.at[i, pair], pair_r.at[i, pair], sibling)
            return carry

        lax.fori_loop(0, NX // 2, pool_pair, 0)

    def finish_row(i):
        for pair in range(NX // 2):
            at = pl.ds(pair * 2, 2)
            pltpu.make_async_remote_copy(
                src_ref=s_send.at[i, at], dst_ref=s_recv.at[i, at], send_sem=pair_s.at[i, pair],
                recv_sem=pair_r.at[i, pair], device_id=sibling, device_id_type=MESH,
            ).wait()
        for d in (2, 1, 3, 0):
            xx = lax.rem(x + d, NX)
            both = s_own[i, xx, 0] + s_recv[i, xx, 0]
            if d == 0:
                acc_a[i] = both
            else:
                pack_rows(both, qa.at[i, d - 1])
                ra_copies[i, d] = send(
                    qa.at[i, d - 1], ra.at[i, d - 1], ra_s.at[i, d - 1], ra_r.at[i, d - 1], at_x(d)
                )
        for d in range(NX):
            xx = lax.rem(x + d, NX)
            both = s_own[i, xx, 1] + s_recv[i, xx, 1]
            if i == 0:
                acc_b[d] = both
            else:
                pack_rows(both, qb.at[i - 1, d])
        if i:
            rb_copies[i] = send(
                qb.at[i - 1], rb.at[i - 1], rb_s.at[i - 1], rb_r.at[i - 1], at_y(row_steps[i])
            )

    pool_row(0)
    for i in range(1, NY):
        info_y[NY - row_steps[i]].wait()
        pool_row(i)
        finish_row(i - 1)
    finish_row(NY - 1)

    before = (
        lax.broadcasted_iota(jnp.int32, (128, 128), 0) < lax.broadcasted_iota(jnp.int32, (128, 128), 1)
    ).astype(F32).astype(BF16)
    ones = jnp.ones((128, 128), BF16)
    block_ids = lax.broadcasted_iota(jnp.int32, (BLKS, 128), 0) + label * BLKS
    low_lanes = lax.broadcasted_iota(jnp.int32, (INFO - SEQ, 128), 1) < Q_DEV
    running = jnp.zeros((BLKS, 128), F32)
    for j in range(2 * TILES):
        tile, p = j // 2, j % 2
        if tile < NY:
            left = info[tile, 2 * p, SEQ:INFO, :].astype(jnp.int32)
            right = info[tile, 2 * p + 1, SEQ:INFO, :].astype(jnp.int32)
            lists = jnp.where(low_lanes, left, pltpu.roll(right, Q_DEV, 1))
        else:
            left = info[2 * p, tile - NY, SEQ:INFO, :].astype(jnp.int32)
            right = info[2 * p + 1, tile - NY, SEQ:INFO, :].astype(jnp.int32)
            lists = jnp.where(low_lanes, pltpu.roll(left, Q_DEV, 1), right)
        hit = jnp.zeros((BLKS, 128), F32)
        place = jnp.zeros((BLKS, 128), F32)
        for k in range(K):
            same = lists[k : k + 1, :] == block_ids
            hit = hit + jnp.where(same, 1.0, 0.0)
            if k < POS:
                at_row = lists[K + k : K + k + 1, :].astype(F32) + 1.0
                place = place + jnp.where(same, at_row, 0.0)
        hit16 = hit.astype(BF16)
        ahead = jnp.dot(hit16, before, preferred_element_type=F32) + running
        running = running + jnp.dot(hit16, ones, preferred_element_type=F32)
        rank[:, j, :] = jnp.where(hit > 0.0, ahead, -1.0)
        off2[:, j, :] = hit + place

    slot_ids = lax.broadcasted_iota(jnp.int32, (GCAP, 128), 0).astype(F32)

    def one_hot(b, carry):
        rows = pl.ds(pl.multiple_of(b * GCAP, GCAP), GCAP)
        found = jnp.zeros((GCAP, 128), F32)
        for j in range(2 * TILES):
            lanes = slice((j % 2) * 128, (j % 2 + 1) * 128)
            same = rank[b, j : j + 1, :] == slot_ids
            onehot[j // 2, rows, lanes] = jnp.where(same, 1.0, 0.0).astype(BF16)
            found = found + jnp.where(same, off2[b, j : j + 1, :], 0.0)
        slot_off[rows, :] = jnp.broadcast_to(jnp.sum(found, axis=1, keepdims=True), (GCAP, 128))
        return carry

    lax.fori_loop(0, BLKS, one_hot, 0)

    second = []
    for i in (1, 2, 3, 0):
        total = acc_a[i]
        for d in (1, 3, 2):
            ra_copies[i, d].wait()
            total = total + unpack_rows(ra.at[i, d - 1])
        if i:
            pack_rows(total, qa2.at[i - 1])
            second.append(
                send(qa2.at[i - 1], ra2.at[i - 1], r2_s.at[0, i - 1], r2_r.at[0, i - 1], at_y(row_steps[i]))
            )
        else:
            acc_a[0] = total
    for i in (1, 2, 3):
        rb_copies[i].wait()
    for d in (2, 1, 3, 0):
        total = acc_b[d]
        for i in range(3):
            total = total + unpack_rows(rb.at[i, d])
        if d:
            pack_rows(total, qb2.at[d - 1])
            second.append(
                send(qb2.at[d - 1], rb2.at[d - 1], r2_s.at[1, d - 1], r2_r.at[1, d - 1], at_x(d))
            )
        else:
            acc_b[0] = total
    for copy in second:
        copy.wait()
    gain = gain_ref[...].reshape(1, D)
    for half in range(2):
        pooled = acc_a[0] if half == 0 else acc_b[0]
        for i in range(3):
            pooled = pooled + unpack_rows(ra2.at[i] if half == 0 else rb2.at[i])
        pooled = pooled / SEQ
        scale = lax.rsqrt(jnp.mean(pooled * pooled, axis=-1, keepdims=True) + 1e-06)
        value = (pooled * scale * gain).astype(BF16)
        if half == 0:
            emb[y, x, c] = value
        else:
            emb[NY + x, y, c] = value

    mine_a, mine_b = emb.at[y, x, c], emb.at[NY + x, y, c]
    ex = {}
    for d in (2, 1, 3):
        ex[0, d] = send(mine_a, mine_a, ex_s.at[0, d - 1], ex_r.at[0, d - 1], at_x(d))
        ex[1, d] = send(mine_b, mine_b, ex_s.at[1, d - 1], ex_r.at[1, d - 1], at_y(d))
    for d in (1, 3, 2):
        ex[0, d].wait()
        ex[1, d].wait()
    row, col = emb.at[y, :, c], emb.at[NY + x, :, c]
    ey = {}
    for d in (2, 1, 3):
        ey[0, d] = send(row, row, ey_s.at[0, d - 1], ey_r.at[0, d - 1], at_y(d))
        ey[1, d] = send(col, col, ey_s.at[1, d - 1], ey_r.at[1, d - 1], at_x(d))

    def forward(d):
        row = emb.at[lax.rem(y + NY - d, NY), :, c]
        col = emb.at[NY + lax.rem(x + NX - d, NX), :, c]
        return [
            send(row, row, es_s.at[0, d], es_r.at[0, d], sibling),
            send(col, col, es_s.at[1, d], es_r.at[1, d], sibling),
        ]

    chunk = SLOTS // 4

    def gather_slots(d, kind):
        tile_a = lax.rem(y + NY - d, NY)
        tile_b = NY + lax.rem(x + NX - d, NX)

        def body(m, carry):
            rows = pl.ds(pl.multiple_of(m * chunk, chunk), chunk)
            value = jnp.dot(
                onehot[tile_a, rows, :], emb[tile_a].reshape(TILE, D), preferred_element_type=F32
            ) + jnp.dot(onehot[tile_b, rows, :], emb[tile_b].reshape(TILE, D), preferred_element_type=F32)
            if kind:
                value = value + eacc[rows, :]
            if kind == 2:
                eslots[rows, :] = value.astype(BF16)
            else:
                eacc[rows, :] = value
            return carry

        lax.fori_loop(0, SLOTS // chunk, body, 0)

    moving = forward(0)
    for n, d in enumerate((1, 3, 2, None)):
        for copy in moving:
            copy.wait()
        if d is not None:
            for half in range(2):
                ey[half, d].wait()
            moving = forward(d)
        gather_slots((0, 1, 3, 2)[n], 0 if n == 0 else 2 if n == 3 else 1)
    load_slab.wait()

    pair_rows = 2 * GCAP
    row_ids = lax.broadcasted_iota(jnp.int32, (pair_rows, 2 * BLOCK), 0)
    col_ids = lax.broadcasted_iota(jnp.int32, (pair_rows, 2 * BLOCK), 1)
    same_block = (row_ids >= GCAP) == (col_ids >= BLOCK)
    col_in = jnp.where(col_ids >= BLOCK, col_ids - BLOCK, col_ids).astype(F32) + 2.0

    def grads(offset):
        dest = lax.rem(z + offset + NZ, NZ)
        srows = pl.ds(pl.multiple_of(dest * pair_rows, pair_rows), pair_rows)
        lrows = pl.ds(pl.multiple_of(dest * 2 * BLOCK, 2 * BLOCK), 2 * BLOCK)
        es_rows = eslots[srows, :]
        labels = slab[lrows, :]
        logits = lax.dot_general(es_rows, labels, (((1,), (1,)), ((), ())), preferred_element_type=F32)
        seen = slot_off[srows, :]
        seen = jnp.concatenate([seen, seen], axis=1)
        g = jax.nn.sigmoid(logits) - jnp.where(seen == col_in, 1.0, 0.0)
        g = jnp.where(same_block & (seen > 0.0), g, 0.0).astype(BF16)
        hgrad[srows, :] = jnp.dot(g, labels, preferred_element_type=F32).astype(BF16)
        return lax.dot_general(g, es_rows, (((0,), (0,)), ((), ())), preferred_element_type=F32)

    zc = {}

    def z_send(way, step, sub):
        zc[way, step, sub] = send(
            zsend.at[way, step, sub], zrecv.at[way, step, sub],
            z_s.at[way, step, sub], z_r.at[way, step, sub], up if way == 0 else down,
        )

    def z_fill(way, step, sub, with_recv):
        value = zpart[way, step - 1, pl.ds(sub * BLOCK, BLOCK), :]
        if with_recv:
            value = value + zrecv[way, step - 1, sub].astype(F32)
        zsend[way, step, sub] = value.astype(BF16)
        z_send(way, step, sub)

    def z_pass(step, first):
        for way in range(2):
            sub = 1 - way if first else way
            zc[way, step - 1, sub].wait()
            z_fill(way, step, sub, True)

    far = grads(4)
    for way in range(2):
        zsend[way, 0, way] = far[way * BLOCK : (way + 1) * BLOCK, :].astype(BF16)
        z_send(way, 0, way)
    for way, sign in ((0, 1), (1, -1)):
        zpart[way, 0] = grads(3 * sign)
        z_fill(way, 1, 1 - way, False)
    for step in (2, 3):
        for way, sign in ((0, 1), (1, -1)):
            zpart[way, step - 1] = grads((4 - step) * sign)
    sg_ref[...] = grads(0)
    z_pass(1, False)

    def spread(tiles):
        def body(k, carry):
            grad = lax.dot_general(
                onehot[k], hgrad[...], (((0,), (0,)), ((), ())), preferred_element_type=F32
            )
            tmp[...] = grad.reshape(4, 2, HALF, D)
            for side in range(4):
                g_own[k, side] = tmp[side, c]
                g_send[k, side] = tmp[side, o].astype(BF16)
            send(g_send.at[k], g_recv.at[k], gp_s.at[k], gp_r.at[k], sibling)
            return carry

        lax.fori_loop(tiles[0], tiles[1], body, 0)

    gx = {}

    def to_chips(k):
        pltpu.make_async_remote_copy(
            src_ref=g_send.at[k], dst_ref=g_recv.at[k], send_sem=gp_s.at[k],
            recv_sem=gp_r.at[k], device_id=sibling, device_id_type=MESH,
        ).wait()
        for d in (2, 1, 3, 0):
            if k < NY:
                piece, device = lax.rem(x + d, NX), at_x(d)
            else:
                piece, device = lax.rem(y + d, NY), at_y(d)
            both = g_own[k, piece] + g_recv[k, piece].astype(F32)
            if d == 0:
                g_own[k, 0] = both
            else:
                gx_send[k, d - 1] = both.astype(BF16)
                gx[k, d] = send(
                    gx_send.at[k, d - 1], gx_recv.at[k, d - 1], gx_s.at[k, d - 1], gx_r.at[k, d - 1], device
                )

    spread((0, 2))
    spread((4, 6))
    z_pass(2, True)
    for k in (0, 4, 1, 5):
        to_chips(k)
    spread((2, 4))
    spread((6, 8))
    z_pass(2, False)
    for k in (2, 6, 3, 7):
        to_chips(k)
    z_pass(3, True)

    def own_total(k):
        total = g_own[k, 0]
        for d in (1, 3, 2):
            total = total + gx_recv[k, d - 1].astype(F32)
        return total

    for k in range(TILES):
        for d in (1, 3, 2):
            gx[k, d].wait()
    z_pass(3, False)
    copies = []
    for d in (2, 1, 3):
        gy_send[0, d - 1] = own_total(lax.rem(y + d, NY))
        copies.append(send(gy_send.at[0, d - 1], gy_recv.at[0, d - 1], gy_s.at[0, d - 1], gy_r.at[0, d - 1], at_y(d)))
        gy_send[1, d - 1] = own_total(NY + lax.rem(x + d, NX))
        copies.append(send(gy_send.at[1, d - 1], gy_recv.at[1, d - 1], gy_s.at[1, d - 1], gy_r.at[1, d - 1], at_x(d)))
    eg_ref[0:HALF, :] = own_total(y)
    eg_ref[HALF:Q_DEV, :] = own_total(NY + x)
    for copy in copies:
        copy.wait()
    for half in range(2):
        rows = pl.ds(half * HALF, HALF)
        eg_ref[rows, :] = eg_ref[rows, :] + gy_recv[half, 0] + gy_recv[half, 1] + gy_recv[half, 2]
    for first in (True, False):
        for way in range(2):
            sub = 1 - way if first else way
            zc[way, 3, sub].wait()
            rows = pl.ds(sub * BLOCK, BLOCK)
            sg_ref[rows, :] = sg_ref[rows, :] + zrecv[way, 3, sub].astype(F32)


def local(token_ids, token_table, norm_gain, slab, shortlist, positive_offsets):
    vmem = pl.BlockSpec(memory_space=pltpu.VMEM)
    anyspace = pl.BlockSpec(memory_space=pl.ANY)
    dma = pltpu.SemaphoreType.DMA
    i16 = jnp.int16
    scratch = dict(
        table=pltpu.VMEM((VOC_PAD, D), BF16),
        slab=pltpu.VMEM((BLKS * BLOCK, D), BF16),
        stage=pltpu.VMEM((INFO, 128), jnp.int32),
        sib_info=pltpu.VMEM((INFO, 128), i16),
        my_info=pltpu.VMEM((INFO, 128), i16),
        info=pltpu.VMEM((NY, NX, INFO, 128), i16),
        lo_ref=pltpu.VMEM((SEQ, 128), jnp.int32),
        w_ref=pltpu.VMEM((SEQ, 128), jnp.int32),
        ct=pltpu.VMEM((VOC_PAD, 256), BF16),
        tmp=pltpu.VMEM((4, 2, HALF, D), F32),
        s_own=pltpu.VMEM((NY, NX, 2, HALF, D), F32),
        s_send=pltpu.VMEM((NY, NX, 2, HALF, D), F32),
        s_recv=pltpu.VMEM((NY, NX, 2, HALF, D), F32),
        qa=pltpu.VMEM((NY, 3, HALF, Q_COLS), i16),
        ra=pltpu.VMEM((NY, 3, HALF, Q_COLS), i16),
        qb=pltpu.VMEM((3, NX, HALF, Q_COLS), i16),
        rb=pltpu.VMEM((3, NX, HALF, Q_COLS), i16),
        qa2=pltpu.VMEM((3, HALF, Q_COLS), i16),
        ra2=pltpu.VMEM((3, HALF, Q_COLS), i16),
        qb2=pltpu.VMEM((3, HALF, Q_COLS), i16),
        rb2=pltpu.VMEM((3, HALF, Q_COLS), i16),
        acc_a=pltpu.VMEM((NY, HALF, D), F32),
        acc_b=pltpu.VMEM((NX, HALF, D), F32),
        emb=pltpu.VMEM((TILES, 4, 2, HALF, D), BF16),
        rank=pltpu.VMEM((BLKS, 2 * TILES, 128), F32),
        off2=pltpu.VMEM((BLKS, 2 * TILES, 128), F32),
        onehot=pltpu.VMEM((TILES, SLOTS, TILE), BF16),
        slot_off=pltpu.VMEM((SLOTS, 128), F32),
        eacc=pltpu.VMEM((SLOTS, D), F32),
        eslots=pltpu.VMEM((SLOTS, D), BF16),
        hgrad=pltpu.VMEM((SLOTS, D), BF16),
        zpart=pltpu.VMEM((2, 3, 2 * BLOCK, D), F32),
        zsend=pltpu.VMEM((2, 4, 2, BLOCK, D), BF16),
        zrecv=pltpu.VMEM((2, 4, 2, BLOCK, D), BF16),
        g_own=pltpu.VMEM((TILES, 4, HALF, D), F32),
        g_send=pltpu.VMEM((TILES, 4, HALF, D), BF16),
        g_recv=pltpu.VMEM((TILES, 4, HALF, D), BF16),
        gx_send=pltpu.VMEM((TILES, 3, HALF, D), BF16),
        gx_recv=pltpu.VMEM((TILES, 3, HALF, D), BF16),
        gy_send=pltpu.VMEM((2, 3, HALF, D), F32),
        gy_recv=pltpu.VMEM((2, 3, HALF, D), F32),
        load_sem=dma((2,)),
        info_s=dma((7,)), info_r=dma((7,)),
        pair_s=dma((NY, 2)), pair_r=dma((NY, 2)),
        ra_s=dma((NY, 3)), ra_r=dma((NY, 3)), rb_s=dma((3,)), rb_r=dma((3,)),
        r2_s=dma((2, 3)), r2_r=dma((2, 3)),
        ex_s=dma((2, 3)), ex_r=dma((2, 3)), ey_s=dma((2, 3)), ey_r=dma((2, 3)),
        es_s=dma((2, 4)), es_r=dma((2, 4)),
        z_s=dma((2, 4, 2)), z_r=dma((2, 4, 2)),
        gp_s=dma((TILES,)), gp_r=dma((TILES,)),
        gx_s=dma((TILES, 3)), gx_r=dma((TILES, 3)), gy_s=dma((2, 3)), gy_r=dma((2, 3)),
    )
    eg, sg = pl.pallas_call(
        kernel,
        out_shape=(
            jax.ShapeDtypeStruct((Q_DEV, D), F32),
            jax.ShapeDtypeStruct((2 * BLOCK, D), F32),
        ),
        in_specs=[vmem, vmem, vmem, vmem, anyspace, anyspace],
        out_specs=(vmem, vmem),
        scratch_shapes=list(scratch.values()),
        compiler_params=pltpu.CompilerParams(
            collective_id=0, has_side_effects=True, vmem_limit_bytes=63 << 20
        ),
    )(token_ids.T, shortlist.T, positive_offsets.T, norm_gain, token_table, slab)
    return eg, sg.reshape(2 * BLOCK, 1, D)


def solution(mesh):
    return jax.shard_map(
        local,
        mesh=mesh,
        in_specs=(
            P(("dp", "label"), None),
            P("label", None),
            P(),
            P("label", None),
            P(("dp", "label"), None),
            P(("dp", "label"), None),
        ),
        out_specs=(P(("dp", "label"), None), P("dp", "label", None)),
        check_vma=False,
    )
```

time: 137 us -> 105 us (0.77)
  Pallas kernels: 126 us -> 100 us
  local copies, waits for them, and re-layouts: 9.89 us -> 4.44 us
    pallas_call x1, Pallas kernels: 126 us -> 100 us  [local(): pl.pallas_call(kernel, out_shape=(jax.ShapeDtypeStruct((Q_DEV, D), F32),...]
    unnamed x5 -> x2, local copies, waits for them, and re-layouts: 8.61 us -> 4.44 us
where the time goes in v2:
time: 105 us
  Pallas kernels  100 us (95%)
  local copies, waits for them, and re-layouts  4.44 us (4%)
    pallas_call x1, Pallas kernels, local(): pl.pallas_call(kernel, out_shape=(jax.ShapeDtypeStruct((Q_DEV, D), F32),...  100 us
    unnamed x2, local copies, waits for them, and re-layouts  4.44 us

profile of v2, /device:TPU:1, one launch (start us, length us, event | category | flops | bytes accessed | tf_op | source)
XLA Modules:
  0.0 105.0 jit_solution(10757081298929604092)
XLA Ops:
  0.6 100.0 %shard_map.77 = (f32[64,768]{1,0:T(8,128)}, f32[256,768]{1,0:T(8,128)}) custom-call(s32[32,64]{1,0:T(8,128)} %bitcast.5, s32[8,64]{1,0:T(8,128)} %bitcast.6, s32[2,64]{1,0:T(2,128)} %bitcast.7, f32[768]{0:T(1024)} %gain_ref.1, bf16[952,768]{1,0:T(8,128)(2,1)} %table_hbm.1, bf16[2048,768]{1,0:T(8,128)(2,1)} %slab_hbm.1), custom_call_target="tpu_custom_call" | custom-call | tf_op jit(solution)/shard_map/pallas_call | solution.py:544
  100.6 2.8 %copy.8 = f32[256,1,768]{2,1,0:T(1,128)} copy(f32[256,1,768]{2,0,1:T(8,128)} %bitcast.4) | data formatting | bytes 1572864
  103.4 1.6 %copy.10 = f32[64,768]{1,0:T(8,128)} copy(f32[64,768]{1,0:T(8,128)} %get-tuple-element.10) | data formatting | bytes 393216

commit v3 on v2

v3 whole, which is shorter than its diff:
```python
import math

import jax
import jax.numpy as jnp
from jax import lax
from jax.experimental import pallas as pl
from jax.experimental.pallas import tpu as pltpu
from jax.sharding import PartitionSpec as P

K = 8
POS = 2
BLOCK = 128
GCAP = 96
SEQ = 32
NX = 4
NY = 4
NZ = 8
CHIPS = NX * NY
Q_DEV = 64
Q_CHIP = 2 * Q_DEV
GROUP = CHIPS * Q_CHIP
VOC = 952
VOC_PAD = 960
LO = 192
FIELDS = 5
D = 768
BLKS = 16
SLOTS = BLKS * GCAP
HALF = Q_DEV // 2
INFO = 48
TILES = 8
TILE = 256
Q_COLS = D + 128
TOP = 32000.0
MESH = pl.DeviceIdType.MESH
F32 = jnp.float32
BF16 = jnp.bfloat16


def pack_rows(value, dst):
    largest = jnp.max(jnp.abs(value), axis=-1, keepdims=True)
    step = jnp.ceil(jnp.log(jnp.maximum(largest, 1e-30)) * (8.0 / math.log(2.0)))
    factor = jnp.exp(step * (-math.log(2.0) / 8.0)) * TOP
    dst[..., 0:D] = jnp.round(value * factor).astype(jnp.int32).astype(jnp.int16)
    dst[..., D:Q_COLS] = jnp.broadcast_to(step, value.shape[:-1] + (128,)).astype(jnp.int32).astype(jnp.int16)


def unpack_rows(src):
    step = src[..., D : D + 1].astype(jnp.int32).astype(F32)
    factor = jnp.exp(step * (math.log(2.0) / 8.0)) * (1.0 / TOP)
    return src[..., 0:D].astype(jnp.int32).astype(F32) * factor


def kernel(
    tok_hbm, list_hbm, pos_hbm, gain_hbm, table_hbm, slab_hbm,
    eg_ref, sg_ref,
    tok_ref, list_ref, pos_ref, gain_ref, table, slab, stage, row_info, info, lo_ref, w_ref, ct, tmp,
    parts, s_recv, keep, q_out, ra, rb, qa2, ra2, qb2, rb2,
    emb, rank, off2, onehot, slot_off, eacc, hgrad,
    zpart, zsend, zrecv,
    g_own, g_send, g_recv, gx_send, gx_recv, gy_send, gy_recv,
    load_sem, info_s, info_r, pair_s, pair_r, ra_s, ra_r, rb_s, rb_r, r2_s, r2_r,
    ex_s, ex_r, ey_s, ey_r, es_s, es_r, z_s, z_r,
    gp_s, gp_r, gx_s, gx_r, gy_s, gy_r,
):
    z = lax.axis_index("dp")
    label = lax.axis_index("label")
    y = lax.div(label, 2 * NX)
    x = lax.rem(lax.div(label, 2), NX)
    c = lax.rem(label, 2)
    o = 1 - c

    def lab(yy, xx, cc):
        return (yy * NX + xx) * 2 + cc

    def at_x(dx):
        return (z, lab(y, lax.rem(x + dx, NX), c))

    def at_y(dy):
        return (z, lab(lax.rem(y + dy, NY), x, c))

    sibling = (z, lab(y, x, o))
    up = (lax.rem(z + 1, NZ), label)
    down = (lax.rem(z + NZ - 1, NZ), label)

    def remote(src, dst, ssem, rsem, device):
        return pltpu.make_async_remote_copy(
            src_ref=src, dst_ref=dst, send_sem=ssem, recv_sem=rsem,
            device_id=device, device_id_type=MESH,
        )

    def send(src, dst, ssem, rsem, device):
        copy = remote(src, dst, ssem, rsem, device)
        copy.start()
        return copy

    barrier = pltpu.get_barrier_semaphore()
    row_peers = [(z, lab(y, lax.rem(x + d, NX), cc)) for d in (2, 1, 3) for cc in (c, o)]
    peers = row_peers + [sibling, up, down] + [at_y(d) for d in (1, 2, 3)]
    for device in peers:
        pl.semaphore_signal(barrier, inc=1, device_id=device, device_id_type=MESH)

    loads = [
        pltpu.make_async_copy(tok_hbm, tok_ref, load_sem.at[2]),
        pltpu.make_async_copy(list_hbm, list_ref, load_sem.at[3]),
        pltpu.make_async_copy(pos_hbm, pos_ref, load_sem.at[4]),
        pltpu.make_async_copy(gain_hbm, gain_ref, load_sem.at[5]),
    ]
    load_table = pltpu.make_async_copy(table_hbm, table.at[pl.ds(0, VOC)], load_sem.at[0])
    load_slab = pltpu.make_async_copy(slab_hbm, slab, load_sem.at[1])
    for load in loads + [load_table, load_slab]:
        load.start()

    stage[...] = jnp.zeros_like(stage)
    for load in loads:
        load.wait()
    for core in range(2):

        @pl.when(c == core)
        def _():
            for half in range(2):
                src = slice(half * HALF, (half + 1) * HALF)
                dst = slice(half * Q_DEV + core * HALF, half * Q_DEV + (core + 1) * HALF)
                stage[0:SEQ, dst] = tok_ref[:, src]
                stage[SEQ : SEQ + K, dst] = list_ref[:, src]
                stage[SEQ + K : SEQ + K + POS, dst] = pos_ref[:, src]

    row_info[0, 0] = stage[...].astype(jnp.int16)
    pl.semaphore_wait(barrier, len(peers))

    copies = []
    for d in (2, 1, 3):
        for s in range(2):
            copies.append(
                send(
                    row_info.at[0, 0], row_info.at[d, s], info_s.at[2 * d + s], info_r.at[2 * d + s],
                    (z, lab(y, lax.rem(x + d, NX), o if s else c)),
                )
            )
    copies.append(send(row_info.at[0, 0], row_info.at[0, 1], info_s.at[1], info_r.at[1], sibling))
    load_table.wait()
    table[VOC:VOC_PAD, :] = jnp.zeros((VOC_PAD - VOC, D), BF16)
    for copy in copies:
        copy.wait()
    for d in range(NX):
        both = row_info[d, 0].astype(jnp.int32) + row_info[d, 1].astype(jnp.int32)
        info[y, lax.rem(x + NX - d, NX)] = both.astype(jnp.int16)

    def info_copy(d):
        return remote(info.at[y], info.at[y], info_s.at[7 + d], info_r.at[7 + d], at_y(d))

    for d in (2, 1, 3):
        info_copy(d).start()

    base = label * VOC
    half_lo = LO // 2
    row_steps = (0, 2, 1, 3)

    def pick(index, values):
        value = values[-1]
        for n in range(len(values) - 2, -1, -1):
            value = jnp.where(index == n, values[n], value)
        return value

    order = [(0, d) for d in (2, 1, 3, 0)] + [(i, d) for i in (1, 2, 3) for d in (2, 1, 3)]
    order += [(i, 0) for i in (1, 2, 3)]
    place_of = {block: divmod(n, 2) for n, block in enumerate(order)}

    def block_of(n):
        rest = jnp.maximum(n - 4, 0)
        i = jnp.where(n < 4, 0, jnp.where(n < 13, 1 + lax.div(rest, 3), n - 12))
        third = jnp.where(n < 4, n, lax.rem(rest, 3))
        d = jnp.where(n >= 13, 0, pick(third, (2, 1, 3, 0)))
        return i, d

    def pair_copy(pair):
        return remote(parts.at[pair, :, o], s_recv.at[pair], pair_s.at[pair], pair_r.at[pair], sibling)

    def ra_copy(i, d, pair, side):
        return remote(q_out.at[pair, 2 * side], ra.at[i, d - 1], ra_s.at[i, d - 1], ra_r.at[i, d - 1], at_x(d))

    def rb_copy(i, d, step, pair, side):
        return remote(
            q_out.at[pair, 2 * side + 1], rb.at[i - 1, d], rb_s.at[i - 1, d], rb_r.at[i - 1, d], at_y(step)
        )

    def pool_pair(pair):
        for side in range(2):
            i, d = block_of(2 * pair + side)
            chip_y, chip_x = lax.rem(y + pick(i, row_steps), NY), lax.rem(x + d, NX)
            ids = info[chip_y, chip_x, 0:SEQ, :].astype(jnp.int32) - base
            valid = (ids >= 0) & (ids < VOC)
            high = (ids * 683) >> 17
            weight = jnp.ones_like(ids)
            for f in range(1, FIELDS):
                weight = jnp.where(high == f, 1 << (6 * f), weight)
            lo_ref[...] = jnp.where(valid, ids - high * LO, -1)
            w_ref[...] = jnp.where(valid, weight, 0)
            for part in range(2):
                rows = lax.broadcasted_iota(jnp.int32, (half_lo, 128), 0) + part * half_lo
                acc = jnp.zeros((half_lo, 128), jnp.int32)
                for t in range(SEQ):
                    acc = acc + jnp.where(lo_ref[t : t + 1, :] == rows, w_ref[t : t + 1, :], 0)
                for f in range(FIELDS):
                    field = (acc >> (6 * f)) & 63
                    ct[pl.ds(f * LO + part * half_lo, half_lo), pl.ds(side * 128, 128)] = (
                        field.astype(F32).astype(BF16)
                    )
        pooled = lax.dot_general(
            ct[...], table[...], (((0,), (0,)), ((), ())), preferred_element_type=F32
        )
        parts[pair] = pooled.reshape(4, 2, HALF, D)
        pair_copy(pair).start()

    def finish_pair(pair):
        pair_copy(pair).wait()
        both = parts[pair, :, c] + s_recv[pair]
        keep[pair] = both
        pack_rows(both, q_out.at[pair])
        for side in range(2):
            i, d = block_of(2 * pair + side)

            @pl.when(d != 0)
            def _():
                ra_copy(i, d, pair, side).start()

            @pl.when(i != 0)
            def _():
                rb_copy(i, d, pick(i, row_steps), pair, side).start()

    def pool_step(pair, carry):
        @pl.when(pair == 2)
        def _():
            info_copy(2).wait()

        @pl.when(pair == 3)
        def _():
            info_copy(3).wait()

        @pl.when(pair == 4)
        def _():
            info_copy(1).wait()

        pool_pair(pair)

        @pl.when(pair > 0)
        def _():
            finish_pair(pair - 1)

        return carry

    lax.fori_loop(0, TILES, pool_step, 0)

    def kept(i, d, half):
        pair, side = place_of[i, d]
        return keep[pair, 2 * side + half]

    second = []
    for d in (2, 1, 3):
        for i in (1, 2, 3):
            rb_copy(i, d, row_steps[i], *place_of[i, d]).wait()
    for d in (2, 1, 3):
        total = kept(0, d, 1)
        for i in (1, 2, 3):
            total = total + unpack_rows(rb.at[i - 1, d])
        pack_rows(total, qb2.at[d - 1])
    for d in (2, 1, 3):
        second.append(send(qb2.at[d - 1], rb2.at[d - 1], r2_s.at[1, d - 1], r2_r.at[1, d - 1], at_x(d)))
    finish_pair(TILES - 1)
    for i in (1, 2, 3):
        for d in (2, 1, 3):
            ra_copy(i, d, *place_of[i, d]).wait()
    for i in (1, 2, 3):
        total = kept(i, 0, 0)
        for d in (1, 3, 2):
            total = total + unpack_rows(ra.at[i, d - 1])
        pack_rows(total, qa2.at[i - 1])
    for i in (1, 2, 3):
        second.append(
            send(qa2.at[i - 1], ra2.at[i - 1], r2_s.at[0, i - 1], r2_r.at[0, i - 1], at_y(row_steps[i]))
        )

    before = (
        lax.broadcasted_iota(jnp.int32, (128, 128), 0) < lax.broadcasted_iota(jnp.int32, (128, 128), 1)
    ).astype(F32).astype(BF16)
    ones = jnp.ones((128, 128), BF16)
    block_ids = lax.broadcasted_iota(jnp.int32, (BLKS, 128), 0) + label * BLKS
    low_lanes = lax.broadcasted_iota(jnp.int32, (INFO - SEQ, 128), 1) < Q_DEV
    running = jnp.zeros((BLKS, 128), F32)
    for j in range(2 * TILES):
        tile, p = j // 2, j % 2
        if tile < NY:
            left = info[tile, 2 * p, SEQ:INFO, :].astype(jnp.int32)
            right = info[tile, 2 * p + 1, SEQ:INFO, :].astype(jnp.int32)
            lists = jnp.where(low_lanes, left, pltpu.roll(right, Q_DEV, 1))
        else:
            left = info[2 * p, tile - NY, SEQ:INFO, :].astype(jnp.int32)
            right = info[2 * p + 1, tile - NY, SEQ:INFO, :].astype(jnp.int32)
            lists = jnp.where(low_lanes, pltpu.roll(left, Q_DEV, 1), right)
        hit = jnp.zeros((BLKS, 128), F32)
        place = jnp.zeros((BLKS, 128), F32)
        for k in range(K):
            same = lists[k : k + 1, :] == block_ids
            hit = hit + jnp.where(same, 1.0, 0.0)
            if k < POS:
                at_row = lists[K + k : K + k + 1, :].astype(F32) + 1.0
                place = place + jnp.where(same, at_row, 0.0)
        hit16 = hit.astype(BF16)
        ahead = jnp.dot(hit16, before, preferred_element_type=F32) + running
        running = running + jnp.dot(hit16, ones, preferred_element_type=F32)
        rank[:, j, :] = jnp.where(hit > 0.0, ahead, -1.0)
        off2[:, j, :] = hit + place

    slot_ids = lax.broadcasted_iota(jnp.int32, (GCAP, 128), 0).astype(F32)

    def one_hot(b, carry):
        rows = pl.ds(pl.multiple_of(b * GCAP, GCAP), GCAP)
        found = jnp.zeros((GCAP, 128), F32)
        for j in range(2 * TILES):
            lanes = slice((j % 2) * 128, (j % 2 + 1) * 128)
            same = rank[b, j : j + 1, :] == slot_ids
            onehot[j // 2, rows, lanes] = jnp.where(same, 1.0, 0.0).astype(BF16)
            found = found + jnp.where(same, off2[b, j : j + 1, :], 0.0)
        slot_off[rows, :] = jnp.broadcast_to(jnp.sum(found, axis=1, keepdims=True), (GCAP, 128))
        return carry

    lax.fori_loop(0, BLKS // 2, one_hot, 0)

    for d in (1, 3, 2):
        ra_copy(0, d, *place_of[0, d]).wait()
    for i in (1, 2, 3):
        rb_copy(i, 0, row_steps[i], *place_of[i, 0]).wait()
    for copy in second:
        copy.wait()
    gain = gain_ref[...].reshape(1, D)
    for half in range(2):
        pooled = kept(0, 0, half)
        for n in range(3):
            pooled = pooled + unpack_rows(ra.at[0, n] if half == 0 else rb.at[n, 0])
            pooled = pooled + unpack_rows(ra2.at[n] if half == 0 else rb2.at[n])
        pooled = pooled / SEQ
        scale = lax.rsqrt(jnp.mean(pooled * pooled, axis=-1, keepdims=True) + 1e-06)
        value = (pooled * scale * gain).astype(BF16)
        if half == 0:
            emb[y, x, c] = value
        else:
            emb[NY + x, y, c] = value

    def ex_copy(half, d):
        mine = emb.at[y, x, c] if half == 0 else emb.at[NY + x, y, c]
        return remote(mine, mine, ex_s.at[half, d - 1], ex_r.at[half, d - 1], at_x(d) if half == 0 else at_y(d))

    def ey_copy(half, back, d):
        if half == 0:
            piece, device = emb.at[y, lax.rem(x + NX - back, NX), c], at_y(d)
        else:
            piece, device = emb.at[NY + x, lax.rem(y + NY - back, NY), c], at_x(d)
        return remote(piece, piece, ey_s.at[half, back, d - 1], ey_r.at[half, back, d - 1], device)

    halves = (0, 1)
    for d in (1, 3, 2):
        for half in halves:
            ex_copy(half, d).start()
    for d in (1, 3, 2):
        for half in halves:
            ey_copy(half, 0, d).start()
    lax.fori_loop(BLKS // 2, BLKS, one_hot, 0)
    for back in (1, 3, 2):
        for half in halves:
            ex_copy(half, back).wait()
            for d in (1, 3):
                ey_copy(half, back, d).start()
    for back in (1, 3, 2):
        for half in halves:
            ey_copy(half, back, 2).start()

    def forward(d):
        row = emb.at[lax.rem(y + NY - d, NY), :, c]
        col = emb.at[NY + lax.rem(x + NX - d, NX), :, c]
        return [
            send(row, row, es_s.at[0, d], es_r.at[0, d], sibling),
            send(col, col, es_s.at[1, d], es_r.at[1, d], sibling),
        ]

    pair_rows = 2 * GCAP
    chunk = SLOTS // 2

    def partial_slots(d, rows):
        tile_a = lax.rem(y + NY - d, NY)
        tile_b = NY + lax.rem(x + NX - d, NX)
        return jnp.dot(
            onehot[tile_a, rows, :], emb[tile_a].reshape(TILE, D), preferred_element_type=F32
        ) + jnp.dot(onehot[tile_b, rows, :], emb[tile_b].reshape(TILE, D), preferred_element_type=F32)

    def gather_slots(d):
        def body(m, carry):
            rows = pl.ds(pl.multiple_of(m * chunk, chunk), chunk)
            value = partial_slots(d, rows)
            eacc[rows, :] = value if d == 0 else value + eacc[rows, :]
            return carry

        lax.fori_loop(0, SLOTS // chunk, body, 0)

    def pieces_wait(d):
        for half in halves:
            for back in range(4):
                ey_copy(half, back, d).wait()

    def all_wait(copies):
        for copy in copies:
            copy.wait()

    moving = forward(0)
    all_wait(moving)
    gather_slots(0)
    pieces_wait(1)
    moving = forward(1)
    pieces_wait(3)
    moving_3 = forward(3)
    all_wait(moving)
    gather_slots(1)
    all_wait(moving_3)
    gather_slots(3)
    pieces_wait(2)
    all_wait(forward(2))
    load_slab.wait()

    row_ids = lax.broadcasted_iota(jnp.int32, (pair_rows, 2 * BLOCK), 0)
    col_ids = lax.broadcasted_iota(jnp.int32, (pair_rows, 2 * BLOCK), 1)
    same_block = (row_ids >= GCAP) == (col_ids >= BLOCK)
    col_in = jnp.where(col_ids >= BLOCK, col_ids - BLOCK, col_ids).astype(F32) + 2.0

    def grads(offset):
        dest = lax.rem(z + offset + NZ, NZ)
        srows = pl.ds(pl.multiple_of(dest * pair_rows, pair_rows), pair_rows)
        lrows = pl.ds(pl.multiple_of(dest * 2 * BLOCK, 2 * BLOCK), 2 * BLOCK)
        es_rows = (partial_slots(2, srows) + eacc[srows, :]).astype(BF16)
        labels = slab[lrows, :]
        logits = lax.dot_general(es_rows, labels, (((1,), (1,)), ((), ())), preferred_element_type=F32)
        seen = slot_off[srows, :]
        seen = jnp.concatenate([seen, seen], axis=1)
        g = jax.nn.sigmoid(logits) - jnp.where(seen == col_in, 1.0, 0.0)
        g = jnp.where(same_block & (seen > 0.0), g, 0.0).astype(BF16)
        hgrad[srows, :] = jnp.dot(g, labels, preferred_element_type=F32).astype(BF16)
        return lax.dot_general(g, es_rows, (((0,), (0,)), ((), ())), preferred_element_type=F32)

    zc = {}

    def z_send(way, step, sub):
        zc[way, step, sub] = send(
            zsend.at[way, step, sub], zrecv.at[way, step, sub],
            z_s.at[way, step, sub], z_r.at[way, step, sub], up if way == 0 else down,
        )

    def z_fill(way, step, sub, with_recv):
        value = zpart[way, step - 1, pl.ds(sub * BLOCK, BLOCK), :]
        if with_recv:
            value = value + zrecv[way, step - 1, sub].astype(F32)
        zsend[way, step, sub] = value.astype(BF16)
        z_send(way, step, sub)

    def z_pass(step, first):
        for way in range(2):
            sub = 1 - way if first else way
            zc[way, step - 1, sub].wait()
            z_fill(way, step, sub, True)

    far = grads(4)
    for way in range(2):
        zsend[way, 0, way] = far[way * BLOCK : (way + 1) * BLOCK, :].astype(BF16)
        z_send(way, 0, way)
    for way, sign in ((0, 1), (1, -1)):
        zpart[way, 0] = grads(3 * sign)
        z_fill(way, 1, 1 - way, False)
    for step in (2, 3):
        for way, sign in ((0, 1), (1, -1)):
            zpart[way, step - 1] = grads((4 - step) * sign)
    sg_ref[...] = grads(0)
    z_pass(1, False)

    def spread(tiles):
        def body(k, carry):
            grad = lax.dot_general(
                onehot[k], hgrad[...], (((0,), (0,)), ((), ())), preferred_element_type=F32
            )
            tmp[...] = grad.reshape(4, 2, HALF, D)
            for side in range(4):
                g_own[k, side] = tmp[side, c]
                g_send[k, side] = tmp[side, o].astype(BF16)
            send(g_send.at[k], g_recv.at[k], gp_s.at[k], gp_r.at[k], sibling)
            return carry

        lax.fori_loop(tiles[0], tiles[1], body, 0)

    gx = {}

    def to_chips(k):
        pltpu.make_async_remote_copy(
            src_ref=g_send.at[k], dst_ref=g_recv.at[k], send_sem=gp_s.at[k],
            recv_sem=gp_r.at[k], device_id=sibling, device_id_type=MESH,
        ).wait()
        for d in (2, 1, 3, 0):
            if k < NY:
                piece, device = lax.rem(x + d, NX), at_x(d)
            else:
                piece, device = lax.rem(y + d, NY), at_y(d)
            both = g_own[k, piece] + g_recv[k, piece].astype(F32)
            if d == 0:
                g_own[k, 0] = both
            else:
                gx_send[k, d - 1] = both.astype(BF16)
                gx[k, d] = send(
                    gx_send.at[k, d - 1], gx_recv.at[k, d - 1], gx_s.at[k, d - 1], gx_r.at[k, d - 1], device
                )

    spread((0, 2))
    spread((4, 6))
    z_pass(2, True)
    for k in (0, 4, 1, 5):
        to_chips(k)
    spread((2, 4))
    spread((6, 8))
    z_pass(2, False)
    for k in (2, 6, 3, 7):
        to_chips(k)
    z_pass(3, True)

    def own_total(k):
        total = g_own[k, 0]
        for d in (1, 3, 2):
            total = total + gx_recv[k, d - 1].astype(F32)
        return total

    for k in range(TILES):
        for d in (1, 3, 2):
            gx[k, d].wait()
    z_pass(3, False)
    copies = []
    for d in (2, 1, 3):
        gy_send[0, d - 1] = own_total(lax.rem(y + d, NY))
        copies.append(send(gy_send.at[0, d - 1], gy_recv.at[0, d - 1], gy_s.at[0, d - 1], gy_r.at[0, d - 1], at_y(d)))
        gy_send[1, d - 1] = own_total(NY + lax.rem(x + d, NX))
        copies.append(send(gy_send.at[1, d - 1], gy_recv.at[1, d - 1], gy_s.at[1, d - 1], gy_r.at[1, d - 1], at_x(d)))
    eg_ref[0:HALF, :] = own_total(y)
    eg_ref[HALF:Q_DEV, :] = own_total(NY + x)
    for copy in copies:
        copy.wait()
    for half in range(2):
        rows = pl.ds(half * HALF, HALF)
        eg_ref[rows, :] = eg_ref[rows, :] + gy_recv[half, 0] + gy_recv[half, 1] + gy_recv[half, 2]
    for first in (True, False):
        for way in range(2):
            sub = 1 - way if first else way
            zc[way, 3, sub].wait()
            rows = pl.ds(sub * BLOCK, BLOCK)
            sg_ref[rows, :] = sg_ref[rows, :] + zrecv[way, 3, sub].astype(F32)


def hand_over(eg_ref, sg_ref, eg_out, sg_out):
    eg_out[...] = eg_ref[...]
    sg_out[...] = sg_ref[...].reshape(2 * BLOCK, 1, D)


def local(token_ids, token_table, norm_gain, slab, shortlist, positive_offsets):
    vmem = pl.BlockSpec(memory_space=pltpu.VMEM)
    anyspace = pl.BlockSpec(memory_space=pl.ANY)
    dma = pltpu.SemaphoreType.DMA
    i16 = jnp.int16
    scratch = dict(
        tok_ref=pltpu.VMEM((SEQ, Q_DEV), jnp.int32),
        list_ref=pltpu.VMEM((K, Q_DEV), jnp.int32),
        pos_ref=pltpu.VMEM((POS, Q_DEV), jnp.int32),
        gain_ref=pltpu.VMEM((D,), F32),
        table=pltpu.VMEM((VOC_PAD, D), BF16),
        slab=pltpu.VMEM((BLKS * BLOCK, D), BF16),
        stage=pltpu.VMEM((INFO, 128), jnp.int32),
        row_info=pltpu.VMEM((NX, 2, INFO, 128), i16),
        info=pltpu.VMEM((NY, NX, INFO, 128), i16),
        lo_ref=pltpu.VMEM((SEQ, 128), jnp.int32),
        w_ref=pltpu.VMEM((SEQ, 128), jnp.int32),
        ct=pltpu.VMEM((VOC_PAD, 256), BF16),
        tmp=pltpu.VMEM((4, 2, HALF, D), F32),
        parts=pltpu.VMEM((TILES, 4, 2, HALF, D), F32),
        s_recv=pltpu.VMEM((TILES, 4, HALF, D), F32),
        keep=pltpu.VMEM((TILES, 4, HALF, D), F32),
        q_out=pltpu.VMEM((TILES, 4, HALF, Q_COLS), i16),
        ra=pltpu.VMEM((NY, 3, HALF, Q_COLS), i16),
        rb=pltpu.VMEM((3, NX, HALF, Q_COLS), i16),
        qa2=pltpu.VMEM((3, HALF, Q_COLS), i16),
        ra2=pltpu.VMEM((3, HALF, Q_COLS), i16),
        qb2=pltpu.VMEM((3, HALF, Q_COLS), i16),
        rb2=pltpu.VMEM((3, HALF, Q_COLS), i16),
        emb=pltpu.VMEM((TILES, 4, 2, HALF, D), BF16),
        rank=pltpu.VMEM((BLKS, 2 * TILES, 128), F32),
        off2=pltpu.VMEM((BLKS, 2 * TILES, 128), F32),
        onehot=pltpu.VMEM((TILES, SLOTS, TILE), BF16),
        slot_off=pltpu.VMEM((SLOTS, 128), F32),
        eacc=pltpu.VMEM((SLOTS, D), F32),
        hgrad=pltpu.VMEM((SLOTS, D), BF16),
        zpart=pltpu.VMEM((2, 3, 2 * BLOCK, D), F32),
        zsend=pltpu.VMEM((2, 4, 2, BLOCK, D), BF16),
        zrecv=pltpu.VMEM((2, 4, 2, BLOCK, D), BF16),
        g_own=pltpu.VMEM((TILES, 4, HALF, D), F32),
        g_send=pltpu.VMEM((TILES, 4, HALF, D), BF16),
        g_recv=pltpu.VMEM((TILES, 4, HALF, D), BF16),
        gx_send=pltpu.VMEM((TILES, 3, HALF, D), BF16),
        gx_recv=pltpu.VMEM((TILES, 3, HALF, D), BF16),
        gy_send=pltpu.VMEM((2, 3, HALF, D), F32),
        gy_recv=pltpu.VMEM((2, 3, HALF, D), F32),
        load_sem=dma((6,)),
        info_s=dma((11,)), info_r=dma((11,)),
        pair_s=dma((TILES,)), pair_r=dma((TILES,)),
        ra_s=dma((NY, 3)), ra_r=dma((NY, 3)), rb_s=dma((3, NX)), rb_r=dma((3, NX)),
        r2_s=dma((2, 3)), r2_r=dma((2, 3)),
        ex_s=dma((2, 3)), ex_r=dma((2, 3)), ey_s=dma((2, 4, 3)), ey_r=dma((2, 4, 3)),
        es_s=dma((2, 4)), es_r=dma((2, 4)),
        z_s=dma((2, 4, 2)), z_r=dma((2, 4, 2)),
        gp_s=dma((TILES,)), gp_r=dma((TILES,)),
        gx_s=dma((TILES, 3)), gx_r=dma((TILES, 3)), gy_s=dma((2, 3)), gy_r=dma((2, 3)),
    )
    eg, sg = pl.pallas_call(
        kernel,
        out_shape=(
            jax.ShapeDtypeStruct((Q_DEV, D), F32),
            jax.ShapeDtypeStruct((2 * BLOCK, D), F32),
        ),
        in_specs=[anyspace] * 6,
        out_specs=(vmem, vmem),
        scratch_shapes=list(scratch.values()),
        compiler_params=pltpu.CompilerParams(
            collective_id=0, has_side_effects=True, vmem_limit_bytes=63 << 20
        ),
    )(token_ids.T, shortlist.T, positive_offsets.T, norm_gain, token_table, slab)
    return pl.pallas_call(
        hand_over,
        out_shape=(
            jax.ShapeDtypeStruct((Q_DEV, D), F32),
            jax.ShapeDtypeStruct((2 * BLOCK, 1, D), F32),
        ),
        in_specs=[vmem, vmem],
        out_specs=(vmem, vmem),
    )(eg, sg)


def solution(mesh):
    return jax.shard_map(
        local,
        mesh=mesh,
        in_specs=(
            P(("dp", "label"), None),
            P("label", None),
            P(),
            P("label", None),
            P(("dp", "label"), None),
            P(("dp", "label"), None),
        ),
        out_specs=(P(("dp", "label"), None), P("dp", "label", None)),
        check_vma=False,
    )
```

time: 105 us -> 95.9 us (0.913)
  Pallas kernels: 100 us -> 95.1 us
  local copies, waits for them, and re-layouts: 4.44 us -> 0 us
    pallas_call x1, Pallas kernels: 100 us -> 92.8 us  [local(): pl.pallas_call(kernel, out_shape=(jax.ShapeDtypeStruct((Q_DEV, D), F32),...]
    unnamed x2 -> x0, local copies, waits for them, and re-layouts: 4.44 us -> none
    pallas_call x0 -> x1, Pallas kernels: none -> 2.29 us  [local(): pl.pallas_call(hand_over, out_shape=(jax.ShapeDtypeStruct((Q_DEV, D), F32...]
where the time goes in v3:
time: 95.9 us; the launch traced here: 95.8 us
  Pallas kernels  95.1 us (99%)
    pallas_call x1, Pallas kernels, local(): pl.pallas_call(kernel, out_shape=(jax.ShapeDtypeStruct((Q_DEV, D), F32),...  92.8 us
    pallas_call x1, Pallas kernels, local(): pl.pallas_call(hand_over, out_shape=(jax.ShapeDtypeStruct((Q_DEV, D), F32...  2.29 us

profile of v3, /device:TPU:1, one launch (start us, length us, event | category | flops | bytes accessed | tf_op | source)
XLA Modules:
  0.0 95.8 jit_solution(689545738646329149)
XLA Ops:
  0.6 92.8 %shard_map.77 = (f32[64,768]{1,0:T(8,128)}, f32[256,768]{1,0:T(8,128)}) custom-call(s32[32,64]{1,0:T(8,128)} %bitcast.3, s32[8,64]{1,0:T(8,128)} %bitcast.4, s32[2,64]{1,0:T(2,128)} %bitcast.5, f32[768]{0:T(1024)} %gain_hbm.1, bf16[952,768]{1,0:T(8,128)(2,1)} %table_hbm.1, bf16[2048,768]{1,0:T(8,128)(2,1)} %slab_hbm.1), custom_call_target="tpu_custom_call" | custom-call | tf_op jit(solution)/shard_map/pallas_call | solution.py:621
  93.5 2.3 %shard_map.78 = (f32[64,768]{1,0:T(8,128)}, f32[256,1,768]{2,1,0:T(1,128)}) custom-call(f32[64,768]{1,0:T(8,128)} %get-tuple-element.4.eg_ref, f32[256,768]{1,0:T(8,128)} %get-tuple-element.5.sg_ref), custom_call_target="tpu_custom_call" | custom-call | tf_op jit(solution)/shard_map/pallas_call | solution.py:634

commit v4 on v3

--- a/solution.py
+++ b/solution.py
@@ -57,10 +57,10 @@
     tok_ref, list_ref, pos_ref, gain_ref, table, slab, stage, row_info, info, lo_ref, w_ref, ct, tmp,
     parts, s_recv, keep, q_out, ra, rb, qa2, ra2, qb2, rb2,
     emb, rank, off2, onehot, slot_off, eacc, hgrad,
-    zpart, zsend, zrecv,
+    zsend, zrecv,
     g_own, g_send, g_recv, gx_send, gx_recv, gy_send, gy_recv,
     load_sem, info_s, info_r, pair_s, pair_r, ra_s, ra_r, rb_s, rb_r, r2_s, r2_r,
-    ex_s, ex_r, ey_s, ey_r, es_s, es_r, z_s, z_r,
+    ex_s, ex_r, ey_s, ey_r, es_s, es_r, ef_s, ef_r, z_s, z_r,
     gp_s, gp_r, gx_s, gx_r, gy_s, gy_r,
 ):
     z = lax.axis_index("dp")
@@ -266,15 +266,13 @@
         pack_rows(total, qb2.at[d - 1])
     for d in (2, 1, 3):
         second.append(send(qb2.at[d - 1], rb2.at[d - 1], r2_s.at[1, d - 1], r2_r.at[1, d - 1], at_x(d)))
-    finish_pair(TILES - 1)
     for i in (1, 2, 3):
         for d in (2, 1, 3):
             ra_copy(i, d, *place_of[i, d]).wait()
+    from_x = [sum(unpack_rows(ra.at[i, d]) for d in range(3)) for i in (1, 2, 3)]
+    finish_pair(TILES - 1)
     for i in (1, 2, 3):
-        total = kept(i, 0, 0)
-        for d in (1, 3, 2):
-            total = total + unpack_rows(ra.at[i, d - 1])
-        pack_rows(total, qa2.at[i - 1])
+        pack_rows(kept(i, 0, 0) + from_x[i - 1], qa2.at[i - 1])
     for i in (1, 2, 3):
         second.append(
             send(qa2.at[i - 1], ra2.at[i - 1], r2_s.at[0, i - 1], r2_r.at[0, i - 1], at_y(row_steps[i]))
@@ -328,16 +326,21 @@
 
     for d in (1, 3, 2):
         ra_copy(0, d, *place_of[0, d]).wait()
+    for copy in second[0:3]:
+        copy.wait()
+    near = [
+        kept(0, 0, 0) + sum(unpack_rows(ra.at[0, n]) for n in range(3)),
+        kept(0, 0, 1) + sum(unpack_rows(rb2.at[n]) for n in range(3)),
+    ]
     for i in (1, 2, 3):
         rb_copy(i, 0, row_steps[i], *place_of[i, 0]).wait()
-    for copy in second:
+    for copy in second[3:6]:
         copy.wait()
     gain = gain_ref[...].reshape(1, D)
     for half in range(2):
-        pooled = kept(0, 0, half)
+        pooled = near[half]
         for n in range(3):
-            pooled = pooled + unpack_rows(ra.at[0, n] if half == 0 else rb.at[n, 0])
-            pooled = pooled + unpack_rows(ra2.at[n] if half == 0 else rb2.at[n])
+            pooled = pooled + unpack_rows(ra2.at[n] if half == 0 else rb.at[n, 0])
         pooled = pooled / SEQ
         scale = lax.rsqrt(jnp.mean(pooled * pooled, axis=-1, keepdims=True) + 1e-06)
         value = (pooled * scale * gain).astype(BF16)
@@ -361,10 +364,10 @@
     for d in (1, 3, 2):
         for half in halves:
             ex_copy(half, d).start()
+    lax.fori_loop(BLKS // 2, BLKS, one_hot, 0)
     for d in (1, 3, 2):
         for half in halves:
             ey_copy(half, 0, d).start()
-    lax.fori_loop(BLKS // 2, BLKS, one_hot, 0)
     for back in (1, 3, 2):
         for half in halves:
             ex_copy(half, back).wait()
@@ -420,9 +423,17 @@
     all_wait(moving)
     gather_slots(1)
     all_wait(moving_3)
+    moving = []
+    for back in (0, 1, 3, 2):
+        for half in halves:
+            ey_copy(half, back, 2).wait()
+            if half == 0:
+                piece = emb.at[lax.rem(y + 2, NY), lax.rem(x + NX - back, NX), c]
+            else:
+                piece = emb.at[NY + lax.rem(x + 2, NX), lax.rem(y + NY - back, NY), c]
+            moving.append(send(piece, piece, ef_s.at[half, back], ef_r.at[half, back], sibling))
     gather_slots(3)
-    pieces_wait(2)
-    all_wait(forward(2))
+    all_wait(moving)
     load_slab.wait()
 
     row_ids = lax.broadcasted_iota(jnp.int32, (pair_rows, 2 * BLOCK), 0)
@@ -453,7 +464,7 @@
         )
 
     def z_fill(way, step, sub, with_recv):
-        value = zpart[way, step - 1, pl.ds(sub * BLOCK, BLOCK), :]
+        value = parts[3 * way + step - 1, pl.ds(2 * sub, 2)].reshape(BLOCK, D)
         if with_recv:
             value = value + zrecv[way, step - 1, sub].astype(F32)
         zsend[way, step, sub] = value.astype(BF16)
@@ -470,11 +481,11 @@
         zsend[way, 0, way] = far[way * BLOCK : (way + 1) * BLOCK, :].astype(BF16)
         z_send(way, 0, way)
     for way, sign in ((0, 1), (1, -1)):
-        zpart[way, 0] = grads(3 * sign)
+        parts[3 * way] = grads(3 * sign).reshape(4, 2, HALF, D)
         z_fill(way, 1, 1 - way, False)
     for step in (2, 3):
         for way, sign in ((0, 1), (1, -1)):
-            zpart[way, step - 1] = grads((4 - step) * sign)
+            parts[3 * way + step - 1] = grads((4 - step) * sign).reshape(4, 2, HALF, D)
     sg_ref[...] = grads(0)
     z_pass(1, False)
 
@@ -537,9 +548,9 @@
     z_pass(3, False)
     copies = []
     for d in (2, 1, 3):
-        gy_send[0, d - 1] = own_total(lax.rem(y + d, NY))
+        pack_rows(own_total(lax.rem(y + d, NY)), gy_send.at[0, d - 1])
         copies.append(send(gy_send.at[0, d - 1], gy_recv.at[0, d - 1], gy_s.at[0, d - 1], gy_r.at[0, d - 1], at_y(d)))
-        gy_send[1, d - 1] = own_total(NY + lax.rem(x + d, NX))
+        pack_rows(own_total(NY + lax.rem(x + d, NX)), gy_send.at[1, d - 1])
         copies.append(send(gy_send.at[1, d - 1], gy_recv.at[1, d - 1], gy_s.at[1, d - 1], gy_r.at[1, d - 1], at_x(d)))
     eg_ref[0:HALF, :] = own_total(y)
     eg_ref[HALF:Q_DEV, :] = own_total(NY + x)
@@ -547,7 +558,7 @@
         copy.wait()
     for half in range(2):
         rows = pl.ds(half * HALF, HALF)
-        eg_ref[rows, :] = eg_ref[rows, :] + gy_recv[half, 0] + gy_recv[half, 1] + gy_recv[half, 2]
+        eg_ref[rows, :] = eg_ref[rows, :] + sum(unpack_rows(gy_recv.at[half, n]) for n in range(3))
     for first in (True, False):
         for way in range(2):
             sub = 1 - way if first else way
@@ -597,7 +608,6 @@
         slot_off=pltpu.VMEM((SLOTS, 128), F32),
         eacc=pltpu.VMEM((SLOTS, D), F32),
         hgrad=pltpu.VMEM((SLOTS, D), BF16),
-        zpart=pltpu.VMEM((2, 3, 2 * BLOCK, D), F32),
         zsend=pltpu.VMEM((2, 4, 2, BLOCK, D), BF16),
         zrecv=pltpu.VMEM((2, 4, 2, BLOCK, D), BF16),
         g_own=pltpu.VMEM((TILES, 4, HALF, D), F32),
@@ -605,15 +615,15 @@
         g_recv=pltpu.VMEM((TILES, 4, HALF, D), BF16),
         gx_send=pltpu.VMEM((TILES, 3, HALF, D), BF16),
         gx_recv=pltpu.VMEM((TILES, 3, HALF, D), BF16),
-        gy_send=pltpu.VMEM((2, 3, HALF, D), F32),
-        gy_recv=pltpu.VMEM((2, 3, HALF, D), F32),
+        gy_send=pltpu.VMEM((2, 3, HALF, Q_COLS), i16),
+        gy_recv=pltpu.VMEM((2, 3, HALF, Q_COLS), i16),
         load_sem=dma((6,)),
         info_s=dma((11,)), info_r=dma((11,)),
         pair_s=dma((TILES,)), pair_r=dma((TILES,)),
         ra_s=dma((NY, 3)), ra_r=dma((NY, 3)), rb_s=dma((3, NX)), rb_r=dma((3, NX)),
         r2_s=dma((2, 3)), r2_r=dma((2, 3)),
         ex_s=dma((2, 3)), ex_r=dma((2, 3)), ey_s=dma((2, 4, 3)), ey_r=dma((2, 4, 3)),
-        es_s=dma((2, 4)), es_r=dma((2, 4)),
+        es_s=dma((2, 4)), es_r=dma((2, 4)), ef_s=dma((2, 4)), ef_r=dma((2, 4)),
         z_s=dma((2, 4, 2)), z_r=dma((2, 4, 2)),
         gp_s=dma((TILES,)), gp_r=dma((TILES,)),
         gx_s=dma((TILES, 3)), gx_r=dma((TILES, 3)), gy_s=dma((2, 3)), gy_r=dma((2, 3)),
@@ -628,7 +638,7 @@
         out_specs=(vmem, vmem),
         scratch_shapes=list(scratch.values()),
         compiler_params=pltpu.CompilerParams(
-            collective_id=0, has_side_effects=True, vmem_limit_bytes=63 << 20
+            collective_id=0, has_side_effects=True, vmem_limit_bytes=57 << 20
         ),
     )(token_ids.T, shortlist.T, positive_offsets.T, norm_gain, token_table, slab)
     return pl.pallas_call(

time: 95.9 us -> 95.5 us (level)
  no operation moved by 1% of the time
where the time goes in v4:
time: 95.5 us; the launch traced here: 95.3 us
  Pallas kernels  94.7 us (99%)
    pallas_call x1, Pallas kernels, local(): pl.pallas_call(kernel, out_shape=(jax.ShapeDtypeStruct((Q_DEV, D), F32),...  92.4 us
    pallas_call x1, Pallas kernels, local(): pl.pallas_call(hand_over, out_shape=(jax.ShapeDtypeStruct((Q_DEV, D), F32...  2.29 us

profile of v4, /device:TPU:1, one launch (start us, length us, event | category | flops | bytes accessed | tf_op | source)
XLA Modules:
  0.0 95.3 jit_solution(9260379036004544436)
XLA Ops:
  0.6 92.4 %shard_map.77 = (f32[64,768]{1,0:T(8,128)}, f32[256,768]{1,0:T(8,128)}) custom-call(s32[32,64]{1,0:T(8,128)} %bitcast.3, s32[8,64]{1,0:T(8,128)} %bitcast.4, s32[2,64]{1,0:T(2,128)} %bitcast.5, f32[768]{0:T(1024)} %gain_hbm.1, bf16[952,768]{1,0:T(8,128)(2,1)} %table_hbm.1, bf16[2048,768]{1,0:T(8,128)(2,1)} %slab_hbm.1), custom_call_target="tpu_custom_call" | custom-call | tf_op jit(solution)/shard_map/pallas_call | solution.py:631
  93.0 2.3 %shard_map.78 = (f32[64,768]{1,0:T(8,128)}, f32[256,1,768]{2,1,0:T(1,128)}) custom-call(f32[64,768]{1,0:T(8,128)} %get-tuple-element.4.eg_ref, f32[256,768]{1,0:T(8,128)} %get-tuple-element.5.sg_ref), custom_call_target="tpu_custom_call" | custom-call | tf_op jit(solution)/shard_map/pallas_call | solution.py:644

commit v5 on v4

--- a/solution.py
+++ b/solution.py
@@ -60,7 +60,7 @@
     zsend, zrecv,
     g_own, g_send, g_recv, gx_send, gx_recv, gy_send, gy_recv,
     load_sem, info_s, info_r, pair_s, pair_r, ra_s, ra_r, rb_s, rb_r, r2_s, r2_r,
-    ex_s, ex_r, ey_s, ey_r, es_s, es_r, ef_s, ef_r, z_s, z_r,
+    ex_s, ex_r, ey_s, ey_r, es_s, es_r, er_s, er_r, ef_s, ef_r, z_s, z_r,
     gp_s, gp_r, gx_s, gx_r, gy_s, gy_r,
 ):
     z = lax.axis_index("dp")
@@ -365,7 +365,7 @@
         for half in halves:
             ex_copy(half, d).start()
     lax.fori_loop(BLKS // 2, BLKS, one_hot, 0)
-    for d in (1, 3, 2):
+    for d in (1, 3):
         for half in halves:
             ey_copy(half, 0, d).start()
     for back in (1, 3, 2):
@@ -373,9 +373,23 @@
             ex_copy(half, back).wait()
             for d in (1, 3):
                 ey_copy(half, back, d).start()
-    for back in (1, 3, 2):
-        for half in halves:
-            ey_copy(half, back, 2).start()
+
+    def relay_copy(half, back, side):
+        rows = pl.ds(side * (HALF // 2), HALF // 2)
+        step = 1 if side == 0 else 3
+        if half == 0:
+            piece = emb.at[lax.rem(y + NY - step, NY), lax.rem(x + NX - back, NX), c, rows]
+            device = at_y(step)
+        else:
+            piece = emb.at[NY + lax.rem(x + NX - step, NX), lax.rem(y + NY - back, NY), c, rows]
+            device = at_x(step)
+        return remote(piece, piece, er_s.at[half, back, side], er_r.at[half, back, side], device)
+
+    def relay(back):
+        for side in range(2):
+            for half in halves:
+                ey_copy(half, back, 1 if side == 0 else 3).wait()
+                relay_copy(half, back, side).start()
 
     def forward(d):
         row = emb.at[lax.rem(y + NY - d, NY), :, c]
@@ -404,21 +418,17 @@
 
         lax.fori_loop(0, SLOTS // chunk, body, 0)
 
-    def pieces_wait(d):
-        for half in halves:
-            for back in range(4):
-                ey_copy(half, back, d).wait()
-
     def all_wait(copies):
         for copy in copies:
             copy.wait()
 
     moving = forward(0)
+    relay(0)
     all_wait(moving)
     gather_slots(0)
-    pieces_wait(1)
+    for back in (1, 3, 2):
+        relay(back)
     moving = forward(1)
-    pieces_wait(3)
     moving_3 = forward(3)
     all_wait(moving)
     gather_slots(1)
@@ -426,7 +436,8 @@
     moving = []
     for back in (0, 1, 3, 2):
         for half in halves:
-            ey_copy(half, back, 2).wait()
+            for side in range(2):
+                relay_copy(half, back, side).wait()
             if half == 0:
                 piece = emb.at[lax.rem(y + 2, NY), lax.rem(x + NX - back, NX), c]
             else:
@@ -445,15 +456,23 @@
         dest = lax.rem(z + offset + NZ, NZ)
         srows = pl.ds(pl.multiple_of(dest * pair_rows, pair_rows), pair_rows)
         lrows = pl.ds(pl.multiple_of(dest * 2 * BLOCK, 2 * BLOCK), 2 * BLOCK)
-        es_rows = (partial_slots(2, srows) + eacc[srows, :]).astype(BF16)
+        es_rows = eacc[srows, :]
+        if offset == 4:
+            es_rows = es_rows + partial_slots(2, srows)
+        es_rows = es_rows.astype(BF16)
         labels = slab[lrows, :]
         logits = lax.dot_general(es_rows, labels, (((1,), (1,)), ((), ())), preferred_element_type=F32)
         seen = slot_off[srows, :]
         seen = jnp.concatenate([seen, seen], axis=1)
         g = jax.nn.sigmoid(logits) - jnp.where(seen == col_in, 1.0, 0.0)
         g = jnp.where(same_block & (seen > 0.0), g, 0.0).astype(BF16)
+        part = lax.dot_general(g, es_rows, (((0,), (0,)), ((), ())), preferred_element_type=F32)
+        if offset == 4:
+            for way in range(2):
+                zsend[way, 0, way] = part[way * BLOCK : (way + 1) * BLOCK, :].astype(BF16)
+                z_send(way, 0, way)
         hgrad[srows, :] = jnp.dot(g, labels, preferred_element_type=F32).astype(BF16)
-        return lax.dot_general(g, es_rows, (((0,), (0,)), ((), ())), preferred_element_type=F32)
+        return part
 
     zc = {}
 
@@ -476,10 +495,8 @@
             zc[way, step - 1, sub].wait()
             z_fill(way, step, sub, True)
 
-    far = grads(4)
-    for way in range(2):
-        zsend[way, 0, way] = far[way * BLOCK : (way + 1) * BLOCK, :].astype(BF16)
-        z_send(way, 0, way)
+    grads(4)
+    gather_slots(2)
     for way, sign in ((0, 1), (1, -1)):
         parts[3 * way] = grads(3 * sign).reshape(4, 2, HALF, D)
         z_fill(way, 1, 1 - way, False)
@@ -554,17 +571,21 @@
         copies.append(send(gy_send.at[1, d - 1], gy_recv.at[1, d - 1], gy_s.at[1, d - 1], gy_r.at[1, d - 1], at_x(d)))
     eg_ref[0:HALF, :] = own_total(y)
     eg_ref[HALF:Q_DEV, :] = own_total(NY + x)
+
+    def ring_end(way, sub):
+        zc[way, 3, sub].wait()
+        rows = pl.ds(sub * BLOCK, BLOCK)
+        sg_ref[rows, :] = sg_ref[rows, :] + zrecv[way, 3, sub].astype(F32)
+
+    for way in range(2):
+        ring_end(way, 1 - way)
     for copy in copies:
         copy.wait()
     for half in range(2):
         rows = pl.ds(half * HALF, HALF)
         eg_ref[rows, :] = eg_ref[rows, :] + sum(unpack_rows(gy_recv.at[half, n]) for n in range(3))
-    for first in (True, False):
-        for way in range(2):
-            sub = 1 - way if first else way
-            zc[way, 3, sub].wait()
-            rows = pl.ds(sub * BLOCK, BLOCK)
-            sg_ref[rows, :] = sg_ref[rows, :] + zrecv[way, 3, sub].astype(F32)
+    for way in range(2):
+        ring_end(way, way)
 
 
 def hand_over(eg_ref, sg_ref, eg_out, sg_out):
@@ -623,7 +644,7 @@
         ra_s=dma((NY, 3)), ra_r=dma((NY, 3)), rb_s=dma((3, NX)), rb_r=dma((3, NX)),
         r2_s=dma((2, 3)), r2_r=dma((2, 3)),
         ex_s=dma((2, 3)), ex_r=dma((2, 3)), ey_s=dma((2, 4, 3)), ey_r=dma((2, 4, 3)),
-        es_s=dma((2, 4)), es_r=dma((2, 4)), ef_s=dma((2, 4)), ef_r=dma((2, 4)),
+        es_s=dma((2, 4)), es_r=dma((2, 4)), er_s=dma((2, 4, 2)), er_r=dma((2, 4, 2)), ef_s=dma((2, 4)), ef_r=dma((2, 4)),
         z_s=dma((2, 4, 2)), z_r=dma((2, 4, 2)),
         gp_s=dma((TILES,)), gp_r=dma((TILES,)),
         gx_s=dma((TILES, 3)), gx_r=dma((TILES, 3)), gy_s=dma((2, 3)), gy_r=dma((2, 3)),

time: 95.5 us -> 92.4 us (0.968)
  Pallas kernels: 94.7 us -> 91.6 us
    pallas_call x1, Pallas kernels: 92.4 us -> 89.3 us  [local(): pl.pallas_call(kernel, out_shape=(jax.ShapeDtypeStruct((Q_DEV, D), F32),...]
where the time goes in v5:
time: 92.4 us; the launch traced here: 92.2 us
  Pallas kernels  91.6 us (99%)
    pallas_call x1, Pallas kernels, local(): pl.pallas_call(kernel, out_shape=(jax.ShapeDtypeStruct((Q_DEV, D), F32),...  89.3 us
    pallas_call x1, Pallas kernels, local(): pl.pallas_call(hand_over, out_shape=(jax.ShapeDtypeStruct((Q_DEV, D), F32...  2.29 us

profile of v5, /device:TPU:1, one launch (start us, length us, event | category | flops | bytes accessed | tf_op | source)
XLA Modules:
  0.0 92.2 jit_solution(7983478007247021377)
XLA Ops:
  0.6 89.3 %shard_map.77 = (f32[64,768]{1,0:T(8,128)}, f32[256,768]{1,0:T(8,128)}) custom-call(s32[32,64]{1,0:T(8,128)} %bitcast.3, s32[8,64]{1,0:T(8,128)} %bitcast.4, s32[2,64]{1,0:T(2,128)} %bitcast.5, f32[768]{0:T(1024)} %gain_hbm.1, bf16[952,768]{1,0:T(8,128)(2,1)} %table_hbm.1, bf16[2048,768]{1,0:T(8,128)(2,1)} %slab_hbm.1), custom_call_target="tpu_custom_call" | custom-call | tf_op jit(solution)/shard_map/pallas_call | solution.py:652
  89.9 2.3 %shard_map.78 = (f32[64,768]{1,0:T(8,128)}, f32[256,1,768]{2,1,0:T(1,128)}) custom-call(f32[64,768]{1,0:T(8,128)} %get-tuple-element.4.eg_ref, f32[256,768]{1,0:T(8,128)} %get-tuple-element.5.sg_ref), custom_call_target="tpu_custom_call" | custom-call | tf_op jit(solution)/shard_map/pallas_call | solution.py:665

commit v6 on v5

--- a/solution.py
+++ b/solution.py
@@ -336,6 +336,10 @@
         rb_copy(i, 0, row_steps[i], *place_of[i, 0]).wait()
     for copy in second[3:6]:
         copy.wait()
+    def ex_copy(half, d):
+        mine = emb.at[y, x, c] if half == 0 else emb.at[NY + x, y, c]
+        return remote(mine, mine, ex_s.at[half, d - 1], ex_r.at[half, d - 1], at_x(d) if half == 0 else at_y(d))
+
     gain = gain_ref[...].reshape(1, D)
     for half in range(2):
         pooled = near[half]
@@ -348,10 +352,8 @@
             emb[y, x, c] = value
         else:
             emb[NY + x, y, c] = value
-
-    def ex_copy(half, d):
-        mine = emb.at[y, x, c] if half == 0 else emb.at[NY + x, y, c]
-        return remote(mine, mine, ex_s.at[half, d - 1], ex_r.at[half, d - 1], at_x(d) if half == 0 else at_y(d))
+        for d in (1, 3, 2):
+            ex_copy(half, d).start()
 
     def ey_copy(half, back, d):
         if half == 0:
@@ -361,9 +363,6 @@
         return remote(piece, piece, ey_s.at[half, back, d - 1], ey_r.at[half, back, d - 1], device)
 
     halves = (0, 1)
-    for d in (1, 3, 2):
-        for half in halves:
-            ex_copy(half, d).start()
     lax.fori_loop(BLKS // 2, BLKS, one_hot, 0)
     for d in (1, 3):
         for half in halves:

time: 92.4 us -> 92.5 us (level)
  no operation moved by 1% of the time
where the time goes in v6:
time: 92.5 us; the launch traced here: 92.3 us
  Pallas kernels  91.7 us (99%)
    pallas_call x1, Pallas kernels, local(): pl.pallas_call(kernel, out_shape=(jax.ShapeDtypeStruct((Q_DEV, D), F32),...  89.4 us
    pallas_call x1, Pallas kernels, local(): pl.pallas_call(hand_over, out_shape=(jax.ShapeDtypeStruct((Q_DEV, D), F32...  2.29 us

profile of v6, /device:TPU:1, one launch (start us, length us, event | category | flops | bytes accessed | tf_op | source)
XLA Modules:
  0.0 92.3 jit_solution(9984191658931974516)
XLA Ops:
  0.6 89.4 %shard_map.77 = (f32[64,768]{1,0:T(8,128)}, f32[256,768]{1,0:T(8,128)}) custom-call(s32[32,64]{1,0:T(8,128)} %bitcast.3, s32[8,64]{1,0:T(8,128)} %bitcast.4, s32[2,64]{1,0:T(2,128)} %bitcast.5, f32[768]{0:T(1024)} %gain_hbm.1, bf16[952,768]{1,0:T(8,128)(2,1)} %table_hbm.1, bf16[2048,768]{1,0:T(8,128)(2,1)} %slab_hbm.1), custom_call_target="tpu_custom_call" | custom-call | tf_op jit(solution)/shard_map/pallas_call | solution.py:651
  90.0 2.3 %shard_map.78 = (f32[64,768]{1,0:T(8,128)}, f32[256,1,768]{2,1,0:T(1,128)}) custom-call(f32[64,768]{1,0:T(8,128)} %get-tuple-element.4.eg_ref, f32[256,768]{1,0:T(8,128)} %get-tuple-element.5.sg_ref), custom_call_target="tpu_custom_call" | custom-call | tf_op jit(solution)/shard_map/pallas_call | solution.py:664
